TPU v7x, 128 devices: a whole 4x4x4 slice. The times are simulated.
128 devices in a mesh: dev: 128 (over y, x, z, core).
Axes of the slice: x: 4, y: 4, z: 4, core: 2. Of those that a mesh axis runs over, the one named last changes fastest.
Arguments:
- node_table: bfloat16 [1048576, 256], P('dev'), may hold values from -6 to 6
- owners: int32 [65536, 2], P('dev'), may hold values from 0 to 127, all different within a row; in each aligned block of 512 rows (0 to 511, 512 to 1023, ...) at most 12 rows name the same one
- local_rows: int32 [65536, 2], P('dev'), may hold values from 0 to 8191
- labels: int32 [65536], P('dev'), may hold values from 0 to 1
- w_first: bfloat16 [768, 512], replicated, may hold values from -0.21875 to 0.21875
- bias_first: float32 [512], replicated, may hold values from -3 to 3
- w_second: bfloat16 [512, 512], replicated, may hold values from -0.25 to 0.25
- bias_second: float32 [512], replicated, may hold values from -3 to 3
- w_head: bfloat16 [512], replicated, may hold values from -0.25 to 0.25
- head_bias: float32 [1], replicated, may hold values from -1 to 1
Outputs:
- new_table: float32 [1048576, 256], P('dev')
- grad_first: float32 [768, 512], replicated
- grad_second: float32 [512, 512], replicated
- grad_small: float32 [3, 512], replicated
Inputs may be any that keep to these rules, and one draw needn't show every extreme that they name: Within each device's 512 pairs no device owns more than 12 endpoints, and some device owns exactly 12; the two endpoints of a pair have different owners.
All inputs are finite; a program needn't handle non-finite values.
Results may differ from a plain program's by a relative error of at most 0.01.
The roundings to bfloat16 on the way count: a program that leaves them out, or rounds other values in their place, can miss the bound.
Values may be sent and summed in bfloat16 or wider, within the bound.
A program may use at most 128 MiB of HBM per device.

v0:
```python
import jax
import jax.numpy as jnp
from jax import lax
from jax.sharding import PartitionSpec as P


def on_device(
    node_table,
    owners,
    local_rows,
    labels,
    w_first,
    bias_first,
    w_second,
    bias_second,
    w_head,
    head_bias,
):
    devices = lax.axis_size("dev")
    rows_dev, emb_width = node_table.shape
    pair_count = owners.shape[0]
    capacity = 3 * pair_count // devices
    flat_owner = owners.reshape(-1)
    flat_row = local_rows.reshape(-1)
    onehot = (flat_owner[:, None] == jnp.arange(devices, dtype=jnp.int32)[None, :]).astype(
        jnp.int32
    )
    in_bucket = jnp.sum((jnp.cumsum(onehot, axis=0) - onehot) * onehot, axis=1)
    slots = flat_owner * capacity + in_bucket
    requests = (
        jnp.zeros((devices * capacity,), jnp.int32)
        .at[slots]
        .set(flat_row)
        .reshape(devices, capacity)
    )
    requested = lax.all_to_all(requests, "dev", split_axis=0, concat_axis=0, tiled=True)
    looked_up = node_table[requested]
    fetched = lax.all_to_all(looked_up, "dev", split_axis=0, concat_axis=0, tiled=True)
    endpoint_rows = fetched.reshape(devices * capacity, emb_width)[slots].reshape(
        pair_count, 2, emb_width
    )
    first_rows = endpoint_rows[:, 0]
    second_rows = endpoint_rows[:, 1]
    product = (first_rows.astype(jnp.float32) * second_rows.astype(jnp.float32)).astype(
        jnp.bfloat16
    )
    features = jnp.concatenate([first_rows, second_rows, product], axis=1)
    pre_first = jnp.dot(features, w_first, preferred_element_type=jnp.float32) + bias_first
    hidden_first = jnp.maximum(pre_first, 0.0).astype(jnp.bfloat16)
    pre_second = jnp.dot(hidden_first, w_second, preferred_element_type=jnp.float32) + bias_second
    hidden_second = jnp.maximum(pre_second, 0.0).astype(jnp.bfloat16)
    logit = jnp.dot(hidden_second, w_head, preferred_element_type=jnp.float32) + head_bias[0]
    dlogit = jax.nn.sigmoid(logit) - labels.astype(jnp.float32)
    delta_second = (
        dlogit[:, None] * w_head.astype(jnp.float32)[None, :] * (pre_second > 0)
    ).astype(jnp.bfloat16)
    delta_first = (
        jnp.dot(delta_second, w_second.T, preferred_element_type=jnp.float32) * (pre_first > 0)
    ).astype(jnp.bfloat16)
    grad_input = jnp.dot(delta_first, w_first.T, preferred_element_type=jnp.float32)
    grad_one = grad_input[:, :emb_width] + grad_input[:, 2 * emb_width :] * second_rows.astype(
        jnp.float32
    )
    grad_two = grad_input[:, emb_width : 2 * emb_width] + grad_input[
        :, 2 * emb_width :
    ] * first_rows.astype(jnp.float32)
    local_first = jnp.dot(features.T, delta_first, preferred_element_type=jnp.float32)
    local_second = jnp.dot(hidden_first.T, delta_second, preferred_element_type=jnp.float32)
    local_small = jnp.stack(
        [
            jnp.sum(delta_first.astype(jnp.float32), axis=0),
            jnp.sum(delta_second.astype(jnp.float32), axis=0),
            jnp.dot(dlogit, hidden_second.astype(jnp.float32)),
        ]
    )
    endpoint_grads = jnp.stack([grad_one, grad_two], axis=1).reshape(2 * pair_count, emb_width)
    outgoing = jnp.zeros((devices * capacity, emb_width), jnp.float32).at[slots].set(endpoint_grads)
    incoming = lax.all_to_all(
        outgoing.reshape(devices, capacity, emb_width),
        "dev",
        split_axis=0,
        concat_axis=0,
        tiled=True,
    )
    row_grad = (
        jnp.zeros((rows_dev, emb_width), jnp.float32)
        .at[requested.reshape(-1)]
        .add(incoming.reshape(devices * capacity, emb_width))
    )
    new_table = node_table.astype(jnp.float32) - 8.0 * row_grad
    grad_first, grad_second, grad_small = lax.psum((local_first, local_second, local_small), "dev")
    return (new_table, grad_first, grad_second, grad_small)


def solution(mesh):
    in_specs = (
        P("dev", None),
        P("dev", None),
        P("dev", None),
        P("dev"),
        P(),
        P(),
        P(),
        P(),
        P(),
        P(),
    )
    out_specs = (P("dev", None), P(), P(), P())
    return jax.shard_map(
        on_device, mesh=mesh, in_specs=in_specs, out_specs=out_specs, check_vma=False
    )
```

profile of v0, /device:TPU:1, one launch (start us, length us, event | category | flops | bytes accessed | tf_op | source)
XLA Modules:
  0.0 273.6 jit_solution(18331449209527925452)
XLA Ops:
  7.2 0.8 broadcast_multiply_fusion
  7.9 0.8 copy.24
  9.6 0.8 copy.28
  11.4 4.3 %scatter_custom_fusion = s32[1536]{0:T(1024)S(1)} fusion(s32[1024]{0:T(1024)S(1)} %bitcast.49, s32[1024]{0:T(1024)S(1)} %reshape.168, s32[]{:T(128)} %constant.8.clone.1), kind=kCustom, calls=%fused_computation.51 | custom fusion | bytes 6148 | tf_op jit(solution)/shard_map/scatter | solution.py:33
  15.8 20.7 %all_to_all.22 = s32[128,1,12]{2,1,0:T(1,128)S(1)} all-to-all(s32[128,1,12]{2,1,0:T(1,128)S(1)} %bitcast.46), channel_id=1, replica_groups=mesh['dev'=128] {'dev'}, dimensions={0} | all-to-all | bytes 12288 | tf_op jit(solution)/shard_map/all_to_all | solution.py:36
  36.6 6.4 %gather_fusion = bf16[1536,256]{1,0:T(8,128)(2,1)S(1)} fusion(bf16[8192,256]{1,0:T(8,128)(2,1)} %param.10, s32[2048]{0:T(1024)S(1)} %pad_clamp_fusion), kind=kCustom, calls=%fused_computation | custom fusion | bytes 1579008 | tf_op jit(solution)/shard_map/gather | solution.py:37
  43.0 1.1 reshape.149
  44.2 4.6 %all-to-all-start.1 = ((bf16[128,12,256]{2,1,0:T(8,128)(2,1)}), bf16[128,12,256]{2,1,0:T(8,128)(2,1)S(1)}, u32[]{:S(2)}, u32[]{:S(2)}) async-start(bf16[128,12,256]{2,1,0:T(8,128)(2,1)} %reshape.149), calls=%async_computation.1 | async-start | bytes 2097152 | tf_op jit(solution)/shard_map/all_to_all | solution.py:38
  49.5 18.6 %all-to-all-done.1 = bf16[128,12,256]{2,1,0:T(8,128)(2,1)S(1)} async-done(((bf16[128,12,256]{2,1,0:T(8,128)(2,1)}), bf16[128,12,256]{2,1,0:T(8,128)(2,1)S(1)}, u32[]{:S(2)}, u32[]{:S(2)}) %all-to-all-start.1) | async-done | bytes 786464 | tf_op jit(solution)/shard_map/all_to_all | solution.py:38
  68.3 3.9 %gather_fusion.1 = bf16[1024,256]{1,0:T(8,128)(2,1)S(1)} fusion(bf16[1536,256]{1,0:T(8,128)(2,1)S(1)} %reshape.143, s32[1024]{0:T(1024)S(1)} %broadcast_clamp_fusion), kind=kCustom, calls=%fused_computation.1 | custom fusion | bytes 1052672 | tf_op jit(solution)/shard_map/gather | solution.py:39
  72.4 0.7 fusion.28
  73.4 0.6 convolution_add_fusion
  74.0 0.6 copy-done.1
  74.6 0.4 convolution_add_fusion.1
  75.6 0.5 convert_reduce_fusion.1
  76.1 0.6 fusion.29
  77.0 1.8 copy.32
  78.8 2.9 %reshape.176 = f32[1024,256]{1,0:T(8,128)} reshape(f32[512,2,256]{2,1,0:T(2,128)} %copy.32) | data formatting | bytes 2097152 | tf_op jit(solution)/shard_map/reshape | solution.py:76
  81.7 6.5 %scatter_custom_fusion.1 = f32[1536,256]{1,0:T(8,128)} fusion(s32[1024]{0:T(1024)S(1)} %bitcast.51, f32[1024,256]{1,0:T(8,128)} %reshape.176, f32[]{:T(128)} %constant.7.clone.1), kind=kCustom, calls=%fused_computation.19 | custom fusion | bytes 1573376 | tf_op jit(solution)/shard_map/scatter | solution.py:77
  88.1 2.6 reshape.146
  90.7 5.7 %all-to-all-start.2 = ((f32[128,12,256]{2,1,0:T(8,128)}), f32[128,12,256]{2,1,0:T(8,128)}, u32[]{:S(2)}, u32[]{:S(2)}) async-start(f32[128,12,256]{2,1,0:T(8,128)} %reshape.146), calls=%async_computation.2 | async-start | bytes 4194304 | tf_op jit(solution)/shard_map/all_to_all | solution.py:78
  96.5 0.5 broadcast.124
  97.0 0.8 reduce.5
  98.0 3.0 %fusion.14 = f32[768,512]{1,0:T(8,128)} fusion(bf16[512,512]{1,0:T(8,128)(2,1)} %copy-done.2, bf16[512,256]{1,0:T(8,128)(2,1)} %copy-done.6, bf16[512,256]{1,0:T(8,128)(2,1)} %copy-done.3, bf16[512,256]{1,0:T(8,128)(2,1)} %copy-done.4), kind=kOutput, calls=%fused_computation.36 | convolution fusion | flops 405012480 | bytes 2883584 | tf_op jit(solution)/shard_map/dot_general | solution.py:67
  101.0 1.4 fusion.16
  102.7 76.6 %psum.23 = f32[3,512]{1,0:T(4,128)} all-reduce(f32[3,512]{1,0:T(4,128)S(1)} %pad_maximum_fusion.4), channel_id=1, replica_groups=mesh['dev'=128] {'dev'}, use_global_device_ids=true, to_apply=%region_10.11 | all-reduce | flops 1536 | bytes 12288 | tf_op jit(solution)/shard_map/psum | solution.py:91
  179.2 1.6 reshape.184
  180.9 12.7 %scatter_custom_fusion.2 = f32[8192,256]{1,0:T(8,128)} fusion(s32[1536]{0:T(1024)S(1)} %fusion.19, f32[1536,256]{1,0:T(8,128)S(1)} %reshape.184, f32[]{:T(128)} %constant.7.clone.1), kind=kCustom, calls=%fused_computation.6 | custom fusion | flops 393216 | bytes 8388612 | tf_op jit(solution)/shard_map/scatter-add | solution.py:88
  193.5 8.8 %multiply_subtract_fusion = f32[8192,256]{1,0:T(8,128)} fusion(f32[8192,256]{1,0:T(8,128)} %scatter_custom_fusion.2, bf16[8192,256]{1,0:T(8,128)(2,1)} %param.10), kind=kLoop, calls=%fused_computation.5 | loop fusion | flops 6291456 | bytes 20971520 | tf_op jit(solution)/shard_map/sub | solution.py:90
  202.3 60.7 %all-reduce.3.cloned.1.call-done = (f32[768,512]{1,0:T(8,128)}, f32[512,512]{1,0:T(8,128)}) async-done(((f32[768,512]{1,0:T(8,128)}, f32[512,512]{1,0:T(8,128)}), (f32[768,512]{1,0:T(8,128)}, f32[512,512]{1,0:T(8,128)})) %all-reduce.3.cloned.1.call-update) | async-done | bytes 2621456 | tf_op jit(solution)/shard_map/psum | solution.py:91
  263.0 2.8 %copy.42 = f32[768,512]{1,0:T(8,128)} copy(f32[768,512]{1,0:T(8,128)} %get-tuple-element.18) | data formatting | bytes 3145728
  265.8 1.0 copy.43
  (57 shorter events, 3.7 us)
Async XLA Ops:
  7.2 66.2 %copy-start = (bf16[768,512]{1,0:T(8,128)(2,1)S(1)}, bf16[768,512]{1,0:T(8,128)(2,1)}, u32[]{:S(2)}) copy-start(bf16[768,512]{1,0:T(8,128)(2,1)} %param.14) | copy-start | bytes 2359300
  43.0 5.8 %copy-start.7 = (bf16[512]{0:T(512)(128)(2,1)S(1)}, bf16[512]{0:T(512)(128)(2,1)}, u32[]{:S(2)}) copy-start(bf16[512]{0:T(512)(128)(2,1)} %param.18) | copy-start | bytes 3076
  44.2 23.9 %all-to-all-start.1 = ((bf16[128,12,256]{2,1,0:T(8,128)(2,1)}), bf16[128,12,256]{2,1,0:T(8,128)(2,1)S(1)}, u32[]{:S(2)}, u32[]{:S(2)}) async-start(bf16[128,12,256]{2,1,0:T(8,128)(2,1)} %reshape.149), calls=%async_computation.1 | async-start | bytes 2097152 | tf_op jit(solution)/shard_map/all_to_all | solution.py:38
  72.4 0.9 copy-start.10
  73.3 0.7 copy-start.6
  73.3 3.4 %copy-start.3 = (bf16[512,256]{1,0:T(8,128)(2,1)}, bf16[512,256]{1,0:T(8,128)(2,1)S(1)}, u32[]{:S(2)}) copy-start(bf16[512,256]{1,0:T(8,128)(2,1)S(1)} %get-tuple-element.9) | copy-start | bytes 786436
  73.3 3.4 %copy-start.4 = (bf16[512,256]{1,0:T(8,128)(2,1)}, bf16[512,256]{1,0:T(8,128)(2,1)S(1)}, u32[]{:S(2)}) copy-start(bf16[512,256]{1,0:T(8,128)(2,1)S(1)} %get-tuple-element.10) | copy-start | bytes 786436
  73.3 1.3 copy-start.1
  73.4 1.3 copy-start.9
  74.6 0.7 copy-start.8
  76.1 0.8 copy-start.2
  90.7 88.5 %all-to-all-start.2 = ((f32[128,12,256]{2,1,0:T(8,128)}), f32[128,12,256]{2,1,0:T(8,128)}, u32[]{:S(2)}, u32[]{:S(2)}) async-start(f32[128,12,256]{2,1,0:T(8,128)} %reshape.146), calls=%async_computation.2 | async-start | bytes 4194304 | tf_op jit(solution)/shard_map/all_to_all | solution.py:78
  96.4 166.6 %all-reduce.3.cloned.1.call-start = ((), (), s32[]{:S(2)}) async-start(), calls=%async_computation.3 | async-start | bytes 5242880 | tf_op jit(solution)/shard_map/psum | solution.py:91
  263.0 2.8 %copy-start.5 = (f32[512,512]{1,0:T(8,128)S(1)}, f32[512,512]{1,0:T(8,128)}, u32[]{:S(2)}) copy-start(f32[512,512]{1,0:T(8,128)} %get-tuple-element.19) | copy-start | bytes 3145732
Sparse Core Ops, SparseCore 0:
  102.9 160.1 all-reduce.2
where the time goes:
time: 274 us
  blocking collectives  97.3 us (36%)
  waiting for transfers between devices  79.3 us (29%)
  local copies, waits for them, and re-layouts  40.3 us (15%)
  other arithmetic  24.4 us (9%)
  between operations  15.1 us (6%)
  starting transfers between devices  10.4 us (4%)
  matrix products  6.98 us (3%)
    psum x1, blocking collectives, on_device(): lax.psum((local_first, local_second, local_small), 'dev')  76.6 us
    psum x1, waiting for transfers between devices, on_device(): lax.psum((local_first, local_second, local_small), 'dev')  60.7 us
    all_to_all x1, blocking collectives, on_device(): lax.all_to_all(requests, 'dev', split_axis=0, concat_axis=0, tiled=True)  20.7 us
    all_to_all x1, waiting for transfers between devices, on_device(): lax.all_to_all(looked_up, 'dev', split_axis=0, concat_axis=0, tiled=True)  18.6 us
    scatter-add x1, other arithmetic, on_device(): row_grad = jnp.zeros((rows_dev, emb_width), jnp.float32).at[requested.res...  12.7 us
    sub x1, other arithmetic, on_device(): new_table = node_table.astype(jnp.float32) - 8.0 * row_grad  8.79 us
    gather x2, local copies, waits for them, and re-layouts, on_device(): looked_up = node_table[requested]  7.52 us
    scatter x1, local copies, waits for them, and re-layouts, on_device(): jnp.zeros((devices * capacity, emb_width), jnp.float32).at[slots]  6.47 us
  transfers between devices with their start and end apart: 3, of which 2 were waited for; matrix products, arithmetic and copies ran while one was open for 11% of the time, Pallas kernels for 0%

commit v1 on v0

v1 whole, which is shorter than its diff:
```python
import jax
import jax.numpy as jnp
from jax import lax
from jax.experimental import pallas as pl
from jax.experimental.pallas import tpu as pltpu
from jax.sharding import PartitionSpec as P

F32, BF16, I32 = jnp.float32, jnp.bfloat16, jnp.int32
MESH = pl.DeviceIdType.MESH
DEVS, CAP = 128, 12
SLOTS = DEVS * CAP
PAIRS, EMB, HID, IN = 512, 256, 512, 768
ROWS = 8192
UNITS, PIECE = 672, 7
UNITS_FIRST, UNITS_SECOND = 384, 256


def nt(a, b):
    return lax.dot_general(a, b, (((1,), (1,)), ((), ())), preferred_element_type=F32)


def tn(a, b):
    return lax.dot_general(a, b, (((0,), (0,)), ((), ())), preferred_element_type=F32)


def dot(a, b):
    return jnp.dot(a, b, preferred_element_type=F32)


def device(y, x, z, c):
    return ((y * 4 + x) * 4 + z) * 2 + c


def far_first(k):
    return 2 + k - 3 * (k // 2) - 2 * (k // 3)


ZC_ORDER = (4, 5, 2, 3, 6, 7, 1, 0)


def remote(src, dst, send, recv, to):
    return pltpu.make_async_remote_copy(
        src_ref=src, dst_ref=dst, send_sem=send, recv_sem=recv, device_id=(to,), device_id_type=MESH
    )


def step_kernel(
    owners, rows, labels, table, w_first, bias_first, w_second, bias_second, w_head, head_bias,
    incoming, row_ids, gathered,
    tab16, tab32, w1, w2,
    ask_send, ask_mid, ask_mid2, ask_got, ask_smem, slot_row, label_col,
    pick, place, stage, rows_send, rows_got, pack, fetched,
    feat, hid1, del1, del2, one_hot_grads, out32, grads_send,
    local32, local16, got_core, sum0, half0, got1, sum1, half1, got2, half2, got3,
    load_sem, ask1_s, ask1_r, ask2_s, ask2_r, smem_sem, row_s, row_r, grad_s, grad_r,
    core_s, core_r, rs1_s, rs1_r, rs2_s, rs2_r, x3_s, x3_r, ag2_s, ag2_r, ag1_s, ag1_r, agc_s, agc_r,
):
    me = lax.axis_index("dev")
    my, mx, mz, mc = me // 32, me // 8 % 4, me // 2 % 4, me % 2

    def zc_plus(j):
        return device(my, mx, (mz + j // 2) % 4, (mc + j) % 2)

    def yx_plus(i):
        return device((my + i // 4) % 4, (mx + i) % 4, mz, mc)

    def minus(i, j):
        return device((my + 4 - i // 4) % 4, (mx + 4 - i % 4) % 4, (mz + 4 - j // 2) % 4, (mc + j) % 2)

    def plus(i, j):
        return device((my + i // 4) % 4, (mx + i) % 4, (mz + j // 2) % 4, (mc + j) % 2)

    barrier = pltpu.get_barrier_semaphore()
    for j in range(1, 8):
        pl.semaphore_signal(barrier, inc=1, device_id=(zc_plus(j),), device_id_type=MESH)
    for i in range(1, 16):
        pl.semaphore_signal(barrier, inc=1, device_id=(yx_plus(i),), device_id_type=MESH)

    loads = [
        pltpu.make_async_copy(
            table.at[pl.ds(k * 2048, 2048)], tab16.at[pl.ds(k * 2048, 2048)], load_sem.at[k]
        )
        for k in range(4)
    ] + [
        pltpu.make_async_copy(w_first, w1, load_sem.at[4]),
        pltpu.make_async_copy(w_second, w2, load_sem.at[5]),
    ]
    for load in loads:
        load.start()

    own = owners[...]
    d_y = ((own >> 5) - my) & 3
    d_x = ((own >> 3) - mx) & 3
    d_z = ((own >> 1) - mz) & 3
    d_c = (own - mc) & 1
    d_yx, d_zc = d_y * 4 + d_x, d_z * 2 + d_c
    ask_bucket, bucket = d_zc * 16 + d_yx, d_yx * 8 + d_zc
    row = rows[...]
    row_hi, row_lo = (row >> 6).astype(F32), (row & 63).astype(F32)
    sub = lax.broadcasted_iota(I32, (128, 128), 0)
    lane = lax.broadcasted_iota(I32, (128, 128), 1)
    earlier = jnp.where(sub < lane, 1.0, 0.0).astype(BF16)
    ones = jnp.ones((128, 128), BF16)
    carry = jnp.zeros((128, 128), F32)
    ask_hi = jnp.zeros((128, 128), F32)
    ask_lo = jnp.zeros((128, 128), F32)
    for b in range(8):
        side, cols = b // 4, slice(128 * (b % 4), 128 * (b % 4) + 128)
        hot32 = jnp.where(sub == ask_bucket[side : side + 1, cols], 1.0, 0.0)
        hot = hot32.astype(BF16)
        before = dot(hot, earlier) + carry
        carry = carry + dot(hot, ones)
        nth = jnp.sum(hot32 * before, axis=0, keepdims=True).astype(I32)
        at_nth = sub == nth
        hi = jnp.where(at_nth, row_hi[side : side + 1, cols], 0.0).astype(BF16)
        lo = jnp.where(at_nth, row_lo[side : side + 1, cols], 0.0).astype(BF16)
        ask_hi = ask_hi + nt(hot, hi)
        ask_lo = ask_lo + nt(hot, lo)
        slot_row[b] = bucket[side : side + 1, cols] * CAP + nth
    ask = (ask_hi * 64.0 + ask_lo).astype(I32)
    for j in range(8):
        ask_send[j] = ask[16 * j : 16 * j + 16]

    pl.semaphore_wait(barrier, 22)
    asks = []
    for j in range(1, 8):
        copy = remote(ask_send.at[j], ask_mid.at[j], ask1_s.at[j], ask1_r.at[j], zc_plus(j))
        copy.start()
        asks.append(copy)
    ask_mid[0] = ask_send[0]

    for k in range(4):
        loads[k].wait()

        @pl.loop(0, 32)
        def _(t):
            at = pl.ds(pl.multiple_of(k * 2048 + t * 64, 64), 64)
            tab32[at, :] = tab16[at, :].astype(F32)

    for copy in asks:
        copy.wait_recv()
    for i in range(16):
        for j in range(8):
            ask_mid2[i, pl.ds(j, 1), :] = ask_mid[j, pl.ds(i, 1), :]
    asks2 = []
    for i in range(1, 16):
        copy = remote(ask_mid2.at[i], ask_got.at[i], ask2_s.at[i], ask2_r.at[i], yx_plus(i))
        copy.start()
        asks2.append(copy)
    ask_got[0] = ask_mid2[0]

    for b in range(8):
        slot_b = slot_row[b]
        column = jnp.transpose(jnp.broadcast_to(slot_b.astype(F32), (128, 128))).astype(I32)

        @pl.loop(0, 12)
        def _(k):
            at = pl.ds(pl.multiple_of(k * 128, 128), 128)
            pick[128 * b : 128 * b + 128, at] = jnp.where(column == lane + k * 128, 1.0, 0.0).astype(BF16)
            place[at, 128 * b : 128 * b + 128] = jnp.where(sub + k * 128 == slot_b, 1.0, 0.0).astype(BF16)

    for b in range(4):
        part = labels[:, 128 * b : 128 * b + 128].astype(F32)
        label_col[128 * b : 128 * b + 128, :] = jnp.transpose(jnp.broadcast_to(part, (128, 128)))

    for copy in asks2:
        copy.wait_recv()
    to_smem = pltpu.make_async_copy(ask_got, ask_smem, smem_sem)
    to_smem.start()
    row_ids[...] = ask_got[...]
    to_smem.wait()

    def look_up(i, j, out):
        for c in range(CAP):
            asked = jnp.clip(ask_smem[i, j, c], 0, ROWS - 1)
            stage[j, pl.ds(c, 1), :] = tab32[pl.ds(asked, 1), :]
        for q in range(3):
            out[q] = stage[j, 4 * q : 4 * q + 4, :].astype(BF16)

    def send_rows(i, j):
        r = i * 8 + j
        look_up(i, j, rows_send.at[r])
        remote(rows_send.at[r], rows_got.at[r], row_s, row_r, minus(i, j)).start()

    def rows_of(t, carry):
        i = far_first(t // 4) * 4 + far_first(t % 4)
        for j in ZC_ORDER:
            send_rows(i, j)
        return carry

    lax.fori_loop(0, 15, rows_of, 0)
    for j in ZC_ORDER[:-1]:
        send_rows(0, j)
    look_up(0, 0, rows_got.at[0])

    for k in (4, 5):
        loads[k].wait()
    rest = pl.ds(1, DEVS - 1)
    pltpu.make_async_copy(rows_got.at[rest], rows_got.at[rest], row_r).wait()

    @pl.loop(0, 32)
    def _(g):
        for a in range(4):
            for q in range(3):
                pack[12 * a + 4 * q : 12 * a + 4 * q + 4, :] = rows_got[g * 4 + a, q].astype(F32)
        fetched[pl.ds(pl.multiple_of(g * 48, 16), 48), :] = pack[...].astype(BF16)

    local32[...] = jnp.zeros_like(local32)
    head = w_head[...].astype(F32)
    small = [jnp.zeros((1, HID), F32)] * 3
    for m in range(2):
        at = slice(256 * m, 256 * m + 256)
        first = dot(pick[256 * m : 256 * m + 256, :], fetched[...])
        second = dot(pick[PAIRS + 256 * m : PAIRS + 256 * m + 256, :], fetched[...])
        feat[at, 0:EMB] = first.astype(BF16)
        feat[at, EMB : 2 * EMB] = second.astype(BF16)
        feat[at, 2 * EMB :] = (first * second).astype(BF16)
        pre_first = dot(feat[at, :], w1[...]) + bias_first[...]
        hid1[at, :] = jnp.maximum(pre_first, 0.0).astype(BF16)
        pre_second = dot(hid1[at, :], w2[...]) + bias_second[...]
        hidden_second = jnp.maximum(pre_second, 0.0).astype(BF16).astype(F32)
        logit = jnp.sum(hidden_second * head, axis=1, keepdims=True) + head_bias[0]
        dlogit = 1.0 / (1.0 + jnp.exp(-logit)) - label_col[at, 0:1]
        delta_second = jnp.where(pre_second > 0, dlogit * head, 0.0).astype(BF16)
        del2[at, :] = delta_second
        delta_first = jnp.where(pre_first > 0, nt(delta_second, w2[...]), 0.0).astype(BF16)
        del1[at, :] = delta_first
        small = [
            small[0] + jnp.sum(delta_first.astype(F32), axis=0, keepdims=True),
            small[1] + jnp.sum(delta_second.astype(F32), axis=0, keepdims=True),
            small[2] + jnp.sum(hidden_second * dlogit, axis=0, keepdims=True),
        ]

    def put(unit, value):
        local32[unit] = value
        local16[unit] = value.astype(BF16)

    for block in range(3):
        grad = tn(feat[:, 256 * block : 256 * block + 256], del1[...])
        for t in range(32):
            for c in range(4):
                put(block * 128 + t * 4 + c, grad[8 * t : 8 * t + 8, 128 * c : 128 * c + 128])
    for block in range(2):
        grad = tn(hid1[:, 256 * block : 256 * block + 256], del2[...])
        for t in range(32):
            for c in range(4):
                put(
                    UNITS_FIRST + block * 128 + t * 4 + c,
                    grad[8 * t : 8 * t + 8, 128 * c : 128 * c + 128],
                )
    for c in range(4):
        for k in range(3):
            local32[640 + c, k : k + 1, :] = small[k][:, 128 * c : 128 * c + 128]
        local16[640 + c] = local32[640 + c].astype(BF16)
    for u in range(644, UNITS):
        local16[u] = jnp.zeros((8, 128), BF16)

    here = {"y": my, "x": mx, "z": mz}

    def along(axis, k):
        at = dict(here)
        at[axis] = (at[axis] + k) % 4
        return device(at["y"], at["x"], at["z"], mc)

    sibling = device(my, mx, mz, 1 - mc)
    lanes = (("y", "x", "z"), ("x", "z", "y"), ("z", "y", "x"))
    span1, span2 = 4 * PIECE, PIECE
    lane_units = 16 * PIECE

    def core_copy(l):
        at = pl.ds((1 - mc) * (UNITS // 2) + l * lane_units, lane_units)
        return remote(local16.at[at], got_core.at[l], core_s.at[l], core_r.at[l], sibling)

    def rs1_copy(l, k):
        axis = lanes[l][0]
        at = pl.ds((here[axis] + k) % 4 * span1, span1)
        return remote(half0.at[l, at], got1.at[l, k], rs1_s.at[l, k], rs1_r.at[l, k], along(axis, k))

    def rs2_copy(l, k):
        axis = lanes[l][1]
        at = pl.ds((here[axis] + k) % 4 * span2, span2)
        return remote(half1.at[l, at], got2.at[l, k], rs2_s.at[l, k], rs2_r.at[l, k], along(axis, k))

    def x3_copy(l, k):
        axis = lanes[l][2]
        return remote(half2.at[l], got3.at[l, here[axis]], x3_s.at[l, k], x3_r.at[l, k], along(axis, k))

    def unit_at(core, l, one, two=0):
        return core * (UNITS // 2) + l * lane_units + one * span1 + two * span2

    def ag2_copy(l, k):
        a, b = here[lanes[l][0]], here[lanes[l][1]]
        at = gathered.at[pl.ds(unit_at(mc, l, a, b), span2)]
        return remote(at, at, ag2_s.at[l, k], ag2_r.at[l, k], along(lanes[l][1], k))

    def ag1_copy(l, k):
        at = gathered.at[pl.ds(unit_at(mc, l, here[lanes[l][0]]), span1)]
        return remote(at, at, ag1_s.at[l, k], ag1_r.at[l, k], along(lanes[l][0], k))

    def agc_copy(l, k):
        at = gathered.at[pl.ds(unit_at(mc, l, (here[lanes[l][0]] + 4 - k) % 4), span1)]
        return remote(at, at, agc_s.at[l, k], agc_r.at[l, k], sibling)

    for l in range(3):
        core_copy(l).start()

    for m in range(2):
        at = slice(256 * m, 256 * m + 256)
        grad_input = nt(del1[at, :], w1[...])
        grad_product = grad_input[:, 2 * EMB :]
        grad_one = grad_input[:, :EMB] + grad_product * feat[at, EMB : 2 * EMB].astype(F32)
        grad_two = grad_input[:, EMB : 2 * EMB] + grad_product * feat[at, 0:EMB].astype(F32)
        one_hot_grads[256 * m : 256 * m + 256, :] = grad_one.astype(BF16)
        one_hot_grads[PAIRS + 256 * m : PAIRS + 256 * m + 256, :] = grad_two.astype(BF16)

    @pl.loop(0, 4)
    def _(k):
        at = pl.ds(pl.multiple_of(k * 384, 128), 384)
        out32[...] = dot(place[at, :], one_hot_grads[...])
        for r in range(32):
            for q in range(3):
                grads_send[k * 32 + r, q] = out32[12 * r + 4 * q : 12 * r + 4 * q + 4, :].astype(BF16)

    for l in range(3):
        core_copy(l).wait_recv()

        @pl.loop(0, 16)
        def _(t):
            at = pl.ds(t * PIECE, PIECE)
            total = (
                local32[pl.ds(mc * (UNITS // 2) + l * lane_units + t * PIECE, PIECE)]
                + got_core[l, at].astype(F32)
            )
            sum0[l, at] = total
            half0[l, at] = total.astype(BF16)

        for k in (2, 1, 3):
            rs1_copy(l, k).start()

    def grad_copy(i, j):
        r = i * 8 + j
        return remote(grads_send.at[r], incoming.at[r], grad_s, grad_r, plus(i, j))

    def grads_of(t, carry):
        i = far_first(t // 4) * 4 + far_first(t % 4)
        for j in ZC_ORDER:
            grad_copy(i, j).start()
        return carry

    lax.fori_loop(0, 15, grads_of, 0)
    for j in ZC_ORDER[:-1]:
        grad_copy(0, j).start()
    incoming[0] = grads_send[0]

    for l in range(3):
        for k in range(1, 4):
            rs1_copy(l, k).wait_recv()
        for t in range(4):
            at = pl.ds(t * PIECE, PIECE)
            total = sum0[l, pl.ds(here[lanes[l][0]] * span1 + t * PIECE, PIECE)]
            for k in range(1, 4):
                total = total + got1[l, k, at].astype(F32)
            sum1[l, at] = total
            half1[l, at] = total.astype(BF16)
        for k in (2, 1, 3):
            rs2_copy(l, k).start()
    for l in range(3):
        for k in range(1, 4):
            rs2_copy(l, k).wait_recv()
        total = sum1[l, pl.ds(here[lanes[l][1]] * span2, PIECE)]
        for k in range(1, 4):
            total = total + got2[l, k].astype(F32)
        half2[l] = total.astype(BF16)
        got3[l, here[lanes[l][2]]] = total.astype(BF16)
        for k in (2, 1, 3):
            x3_copy(l, k).start()
    for l in range(3):
        for k in range(1, 4):
            x3_copy(l, k).wait_recv()
        total = got3[l, 0].astype(F32)
        for a in range(1, 4):
            total = total + got3[l, a].astype(F32)
        gathered[pl.ds(unit_at(mc, l, here[lanes[l][0]], here[lanes[l][1]]), PIECE)] = total.astype(BF16)
        for k in (2, 1, 3):
            ag2_copy(l, k).start()
    for l in range(3):
        for k in range(1, 4):
            ag2_copy(l, k).wait_recv()
        for k in (2, 1, 3):
            ag1_copy(l, k).start()
        agc_copy(l, 0).start()
    for l in range(3):
        for k in (1, 3, 2):
            ag1_copy(l, k).wait_recv()
            agc_copy(l, k).start()
    for l in range(3):
        for k in range(4):
            agc_copy(l, k).wait_recv()
    pltpu.make_async_copy(incoming.at[rest], incoming.at[rest], grad_r).wait()

    for copy in asks + asks2:
        copy.wait_send()
    pltpu.make_async_copy(rows_send.at[rest], rows_send.at[rest], row_s).wait()
    pltpu.make_async_copy(grads_send.at[rest], grads_send.at[rest], grad_s).wait()
    for l in range(3):
        core_copy(l).wait_send()
        for k in range(1, 4):
            for copy in (rs1_copy, rs2_copy, x3_copy, ag2_copy, ag1_copy):
                copy(l, k).wait_send()
        for k in range(4):
            agc_copy(l, k).wait_send()


def step(owners, rows, labels, table, w_first, bias_first, w_second, bias_second, w_head, head_bias):
    vmem = pl.BlockSpec(memory_space=pltpu.VMEM)
    any_ = pl.BlockSpec(memory_space=pl.ANY)
    dma = pltpu.SemaphoreType.DMA
    scratch = [
        pltpu.VMEM((ROWS, EMB), BF16),
        pltpu.VMEM((ROWS, EMB), F32),
        pltpu.VMEM((IN, HID), BF16),
        pltpu.VMEM((HID, HID), BF16),
        pltpu.VMEM((8, 16, 128), I32),
        pltpu.VMEM((8, 16, 128), I32),
        pltpu.VMEM((16, 8, 128), I32),
        pltpu.VMEM((16, 8, 128), I32),
        pltpu.SMEM((16, 8, 128), I32),
        pltpu.VMEM((8, 1, 128), I32),
        pltpu.VMEM((PAIRS, 128), F32),
        pltpu.VMEM((2 * PAIRS, SLOTS), BF16),
        pltpu.VMEM((SLOTS, 2 * PAIRS), BF16),
        pltpu.VMEM((8, 16, EMB), F32),
        pltpu.VMEM((DEVS, 3, 4, EMB), BF16),
        pltpu.VMEM((DEVS, 3, 4, EMB), BF16),
        pltpu.VMEM((48, EMB), F32),
        pltpu.VMEM((SLOTS, EMB), BF16),
        pltpu.VMEM((PAIRS, IN), BF16),
        pltpu.VMEM((PAIRS, HID), BF16),
        pltpu.VMEM((PAIRS, HID), BF16),
        pltpu.VMEM((PAIRS, HID), BF16),
        pltpu.VMEM((2 * PAIRS, EMB), BF16),
        pltpu.VMEM((384, EMB), F32),
        pltpu.VMEM((DEVS, 3, 4, EMB), BF16),
        pltpu.VMEM((UNITS, 8, 128), F32),
        pltpu.VMEM((UNITS, 8, 128), BF16),
        pltpu.VMEM((3, 16 * PIECE, 8, 128), BF16),
        pltpu.VMEM((3, 16 * PIECE, 8, 128), F32),
        pltpu.VMEM((3, 16 * PIECE, 8, 128), BF16),
        pltpu.VMEM((3, 4, 4 * PIECE, 8, 128), BF16),
        pltpu.VMEM((3, 4 * PIECE, 8, 128), F32),
        pltpu.VMEM((3, 4 * PIECE, 8, 128), BF16),
        pltpu.VMEM((3, 4, PIECE, 8, 128), BF16),
        pltpu.VMEM((3, PIECE, 8, 128), BF16),
        pltpu.VMEM((3, 4, PIECE, 8, 128), BF16),
        dma((6,)), dma((8,)), dma((8,)), dma((16,)), dma((16,)), dma, dma, dma, dma, dma,
        dma((3,)), dma((3,)), dma((3, 4)), dma((3, 4)), dma((3, 4)), dma((3, 4)), dma((3, 4)), dma((3, 4)),
        dma((3, 4)), dma((3, 4)), dma((3, 4)), dma((3, 4)), dma((3, 4)), dma((3, 4)),
    ]
    return pl.pallas_call(
        step_kernel,
        out_shape=(
            jax.ShapeDtypeStruct((DEVS, 3, 4, EMB), BF16),
            jax.ShapeDtypeStruct((16, 8, 128), I32),
            jax.ShapeDtypeStruct((UNITS, 8, 128), BF16),
        ),
        in_specs=[vmem, vmem, vmem, any_, any_, vmem, any_, vmem, vmem, pl.BlockSpec(memory_space=pltpu.SMEM)],
        out_specs=(vmem, vmem, vmem),
        scratch_shapes=scratch,
        compiler_params=pltpu.CompilerParams(
            collective_id=0, has_side_effects=True, vmem_limit_bytes=56 << 20
        ),
        name="exchange_and_mlp",
    )(owners, rows, labels, table, w_first, bias_first, w_second, bias_second, w_head, head_bias)


BLOCK = 1024


def update_kernel(
    table, incoming, ids, units_first, units_second, units_small,
    new_table, grad_first, grad_second, grad_small,
    pack, grads,
):
    step = pl.program_id(0)

    @pl.when(step == 0)
    def _():
        @pl.loop(0, 32)
        def _(g):
            for a in range(4):
                for q in range(3):
                    pack[12 * a + 4 * q : 12 * a + 4 * q + 4, :] = incoming[g * 4 + a, q].astype(F32)
            grads[pl.ds(pl.multiple_of(g * 48, 16), 48), :] = pack[...].astype(BF16)

    for c in range(4):
        for t in range(12):
            grad_first[8 * t : 8 * t + 8, 128 * c : 128 * c + 128] = units_first[4 * t + c].astype(F32)
        for t in range(8):
            grad_second[8 * t : 8 * t + 8, 128 * c : 128 * c + 128] = units_second[4 * t + c].astype(F32)
        grad_small[:, 128 * c : 128 * c + 128] = units_small[c].astype(F32)[0:3]

    @pl.loop(0, BLOCK // 256)
    def _(t):
        at = pl.ds(pl.multiple_of(t * 256, 256), 256)
        here = lax.broadcasted_iota(I32, (256, SLOTS), 0) + (step * BLOCK + t * 256)
        hot = jnp.where(here == ids[...], 1.0, 0.0).astype(BF16)
        new_table[at, :] = table[at, :].astype(F32) - 8.0 * dot(hot, grads[...])


def update(table, incoming, ids, units):
    steps = ROWS // BLOCK
    return pl.pallas_call(
        update_kernel,
        grid=(steps,),
        in_specs=[
            pl.BlockSpec((BLOCK, EMB), lambda s: (s, 0)),
            pl.BlockSpec((DEVS, 3, 4, EMB), lambda s: (0, 0, 0, 0)),
            pl.BlockSpec((1, SLOTS), lambda s: (0, 0)),
            pl.BlockSpec((UNITS_FIRST // steps, 8, 128), lambda s: (s, 0, 0)),
            pl.BlockSpec((UNITS_SECOND // steps, 8, 128), lambda s: (12 + s, 0, 0)),
            pl.BlockSpec((4, 8, 128), lambda s: (160, 0, 0)),
        ],
        out_specs=(
            pl.BlockSpec((BLOCK, EMB), lambda s: (s, 0)),
            pl.BlockSpec((IN // steps, HID), lambda s: (s, 0)),
            pl.BlockSpec((HID // steps, HID), lambda s: (s, 0)),
            pl.BlockSpec((3, HID), lambda s: (0, 0)),
        ),
        out_shape=(
            jax.ShapeDtypeStruct((ROWS, EMB), F32),
            jax.ShapeDtypeStruct((IN, HID), F32),
            jax.ShapeDtypeStruct((HID, HID), F32),
            jax.ShapeDtypeStruct((3, HID), F32),
        ),
        scratch_shapes=[pltpu.VMEM((48, EMB), F32), pltpu.VMEM((SLOTS, EMB), BF16)],
        compiler_params=pltpu.CompilerParams(vmem_limit_bytes=48 << 20),
        name="scatter_update",
    )(table, incoming, ids, units, units, units)


def on_device(
    node_table, owners, local_rows, labels, w_first, bias_first, w_second, bias_second, w_head, head_bias
):
    incoming, row_ids, units = step(
        owners.T, local_rows.T, labels.reshape(1, PAIRS), node_table,
        w_first, bias_first.reshape(1, HID), w_second, bias_second.reshape(1, HID),
        w_head.reshape(1, HID), head_bias,
    )
    ids = row_ids[:, :, :CAP].reshape(1, SLOTS)
    return update(node_table, incoming, ids, units)


def solution(mesh):
    in_specs = (P("dev", None), P("dev", None), P("dev", None), P("dev"), P(), P(), P(), P(), P(), P())
    out_specs = (P("dev", None), P(), P(), P())
    return jax.shard_map(on_device, mesh=mesh, in_specs=in_specs, out_specs=out_specs, check_vma=False)
```

time: 274 us -> 93.2 us (0.34)
  blocking collectives: 97.3 us -> 0 us
  Pallas kernels: 0 us -> 87 us
  waiting for transfers between devices: 79.3 us -> 0 us
  local copies, waits for them, and re-layouts: 40.3 us -> 4.67 us
  other arithmetic: 24.4 us -> 0 us
  between operations: 15.1 us -> 1.3 us
  starting transfers between devices: 10.4 us -> 0 us
  matrix products: 6.98 us -> 0 us
    pallas_call x0 -> x2, Pallas kernels: none -> 87 us  [the longest x1 71.8 us: step(): pl.pallas_call(step_kernel, out_shape=(jax.ShapeDtypeStruct((DEVS, 3, 4,...]
    psum x1 -> x0, blocking collectives: 76.6 us -> none  [on_device(): lax.psum((local_first, local_second, local_small), 'dev')]
    psum x1 -> x0, waiting for transfers between devices: 60.7 us -> none  [on_device(): lax.psum((local_first, local_second, local_small), 'dev')]
    all_to_all x1 -> x0, blocking collectives: 20.7 us -> none  [on_device(): lax.all_to_all(requests, 'dev', split_axis=0, concat_axis=0, tiled=True)]
    all_to_all x2 -> x0, waiting for transfers between devices: 18.6 us -> none  [the longest x1 18.6 us: on_device(): lax.all_to_all(looked_up, 'dev', split_axis=0, concat_axis=0, tiled=True)]
    scatter-add x1 -> x0, other arithmetic: 12.7 us -> none  [on_device(): row_grad = jnp.zeros((rows_dev, emb_width), jnp.float32).at[requested.res...]
    gather x3 -> x0, local copies, waits for them, and re-layouts: 11.5 us -> none  [the longest x2 7.52 us: on_device(): looked_up = node_table[requested]]
    scatter x2 -> x0, local copies, waits for them, and re-layouts: 10.8 us -> none  [the longest x1 6.47 us: on_device(): jnp.zeros((devices * capacity, emb_width), jnp.float32).at[slots]]
  transfers between devices with their start and end apart: 3 -> 0, of which waited for: 2 -> 0; matrix products, arithmetic and copies ran while one was open for 11% -> 0% of each run, Pallas kernels for 0% -> 0%
where the time goes in v1:
time: 93.2 us; the launch traced here: 92.9 us
  Pallas kernels  87 us (93%)
  local copies, waits for them, and re-layouts  4.67 us (5%)
  between operations  1.3 us (1%)
    pallas_call x1, Pallas kernels, step(): pl.pallas_call(step_kernel, out_shape=(jax.ShapeDtypeStruct((DEVS, 3, 4,...  71.8 us
    pallas_call x1, Pallas kernels, update(): pl.pallas_call(update_kernel, grid=(steps,), in_specs=[pl.BlockSpec((BLOC...  15.2 us
    unnamed x4, local copies, waits for them, and re-layouts  2.47 us

profile of v1, /device:TPU:1, one launch (start us, length us, event | category | flops | bytes accessed | tf_op | source)
XLA Modules:
  0.0 92.9 jit_solution(4899304540320646003)
XLA Ops:
  1.3 1.3 %reshape.26.w_head = bf16[1,512]{1,0:T(2,128)(2,1)} reshape(bf16[512]{0:T(512)(128)(2,1)} %param.18) | data formatting | bytes 2048 | tf_op jit(solution)/shard_map/reshape | solution.py:547
  2.5 71.8 %exchange_and_mlp.1 = (bf16[128,3,4,256]{3,2,1,0:T(4,128)(2,1)}, s32[16,8,128]{2,1,0:T(8,128)}, bf16[672,8,128]{2,1,0:T(8,128)(2,1)}) custom-call(s32[2,512]{1,0:T(2,128)} %bitcast.7, s32[2,512]{1,0:T(2,128)} %bitcast.8, s32[1,512]{1,0:T(1,128)} %bitcast.9, bf16[8192,256]{1,0:T(8,128)(2,1)} %table.3, bf16[768,512]{1,0:T(8,128)(2,1)} %w_first.1, ...), custom_call_target="tpu_custom_call" | custom-call | tf_op jit(solution)/shard_map/exchange_and_mlp/pallas_call | solution.py:459
  74.3 0.9 %reshape.27.ids = s32[1,1536]{1,0:T(1,128)S(1)} reshape(s32[16,8,12]{2,1,0:T(8,128)} %bitcast.6) | data formatting | bytes 12288 | tf_op jit(solution)/shard_map/reshape | solution.py:549
  75.3 0.0 copy-start
  75.3 1.3 %copy-done = bf16[672,8,128]{2,1,0:T(8,128)(2,1)S(1)} copy-done((bf16[672,8,128]{2,1,0:T(8,128)(2,1)S(1)}, bf16[672,8,128]{2,1,0:T(8,128)(2,1)}, u32[]{:S(2)}) %copy-start) | copy-done | bytes 1376280
  76.6 0.0 copy-start.1
  76.6 1.1 %copy-done.1 = bf16[128,3,4,256]{3,2,1,0:T(4,128)(2,1)S(1)} copy-done((bf16[128,3,4,256]{3,2,1,0:T(4,128)(2,1)S(1)}, bf16[128,3,4,256]{3,2,1,0:T(4,128)(2,1)}, u32[]{:S(2)}) %copy-start.1) | copy-done | bytes 786456
  77.8 15.2 %scatter_update.1 = (f32[8192,256]{1,0:T(8,128)}, f32[768,512]{1,0:T(8,128)}, f32[512,512]{1,0:T(8,128)}, f32[3,512]{1,0:T(4,128)}) custom-call(bf16[8192,256]{1,0:T(8,128)(2,1)} %table.3, bf16[128,3,4,256]{3,2,1,0:T(4,128)(2,1)S(1)} %copy-done.1, s32[1,1536]{1,0:T(1,128)S(1)} %reshape.27.ids, bf16[672,8,128]{2,1,0:T(8,128)(2,1)S(1)} %copy-done, ...), custom_call_target="tpu_custom_call" | custom-call | tf_op jit(solution)/shard_map/scatter_update/pallas_call | solution.py:512
Async XLA Ops:
  75.3 1.3 %copy-start = (bf16[672,8,128]{2,1,0:T(8,128)(2,1)S(1)}, bf16[672,8,128]{2,1,0:T(8,128)(2,1)}, u32[]{:S(2)}) copy-start(bf16[672,8,128]{2,1,0:T(8,128)(2,1)} %get-tuple-element.9.units_first.units_second.units_small) | copy-start | bytes 4128772
  76.6 1.1 %copy-start.1 = (bf16[128,3,4,256]{3,2,1,0:T(4,128)(2,1)S(1)}, bf16[128,3,4,256]{3,2,1,0:T(4,128)(2,1)}, u32[]{:S(2)}) copy-start(bf16[128,3,4,256]{3,2,1,0:T(4,128)(2,1)} %get-tuple-element.7.incoming) | copy-start | bytes 2359300

commit v2 on v1

--- a/solution.py
+++ b/solution.py
@@ -13,6 +13,7 @@
 ROWS = 8192
 UNITS, PIECE = 672, 7
 UNITS_FIRST, UNITS_SECOND = 384, 256
+VMEM_STEP = 50 << 20
 
 
 def nt(a, b):
@@ -46,8 +47,8 @@
 
 def step_kernel(
     owners, rows, labels, table, w_first, bias_first, w_second, bias_second, w_head, head_bias,
-    incoming, row_ids, gathered,
-    tab16, tab32, w1, w2,
+    tab32, gathered,
+    incoming, row_ids, hot_rows, tab16, w1, w2,
     ask_send, ask_mid, ask_mid2, ask_got, ask_smem, slot_row, label_col,
     pick, place, stage, rows_send, rows_got, pack, fetched,
     feat, hid1, del1, del2, one_hot_grads, out32, grads_send,
@@ -69,6 +70,17 @@
 
     def plus(i, j):
         return device((my + i // 4) % 4, (mx + i) % 4, (mz + j // 2) % 4, (mc + j) % 2)
+
+    sent = []
+
+    def flush():
+        for wait in sent:
+            wait()
+
+    def start(copy):
+        copy.start()
+        sent.append(copy.wait_send)
+        return copy
 
     barrier = pltpu.get_barrier_semaphore()
     for j in range(1, 8):
@@ -101,32 +113,33 @@
     lane = lax.broadcasted_iota(I32, (128, 128), 1)
     earlier = jnp.where(sub < lane, 1.0, 0.0).astype(BF16)
     ones = jnp.ones((128, 128), BF16)
+    in_lane = jnp.where(sub < 8 * CAP, sub % CAP, -1)
+
+    def part(array, b):
+        return array[b // 4 : b // 4 + 1, 128 * (b % 4) : 128 * (b % 4) + 128]
+
+    hots32 = [jnp.where(sub == part(ask_bucket, b), 1.0, 0.0) for b in range(8)]
+    hots = [hot.astype(BF16) for hot in hots32]
+    counts = dot(jnp.concatenate(hots, axis=0), jnp.concatenate([earlier, ones], axis=1))
     carry = jnp.zeros((128, 128), F32)
-    ask_hi = jnp.zeros((128, 128), F32)
-    ask_lo = jnp.zeros((128, 128), F32)
+    values = []
     for b in range(8):
-        side, cols = b // 4, slice(128 * (b % 4), 128 * (b % 4) + 128)
-        hot32 = jnp.where(sub == ask_bucket[side : side + 1, cols], 1.0, 0.0)
-        hot = hot32.astype(BF16)
-        before = dot(hot, earlier) + carry
-        carry = carry + dot(hot, ones)
-        nth = jnp.sum(hot32 * before, axis=0, keepdims=True).astype(I32)
-        at_nth = sub == nth
-        hi = jnp.where(at_nth, row_hi[side : side + 1, cols], 0.0).astype(BF16)
-        lo = jnp.where(at_nth, row_lo[side : side + 1, cols], 0.0).astype(BF16)
-        ask_hi = ask_hi + nt(hot, hi)
-        ask_lo = ask_lo + nt(hot, lo)
-        slot_row[b] = bucket[side : side + 1, cols] * CAP + nth
-    ask = (ask_hi * 64.0 + ask_lo).astype(I32)
+        before = counts[128 * b : 128 * b + 128, :128] + carry
+        carry = carry + counts[128 * b : 128 * b + 128, 128:]
+        nth = jnp.sum(hots32[b] * before, axis=0, keepdims=True).astype(I32)
+        hi = jnp.where(in_lane == nth, part(row_hi, b), 0.0).astype(BF16)
+        lo = jnp.where(in_lane == nth, part(row_lo, b), 0.0).astype(BF16)
+        values.append(jnp.concatenate([hi, lo], axis=0))
+        slot_row[b] = part(bucket, b) * CAP + nth
+    halves = nt(jnp.concatenate(hots, axis=1), jnp.concatenate(values, axis=1))
+    ask = (halves[:, :128] * 64.0 + halves[:, 128:]).astype(I32)
     for j in range(8):
         ask_send[j] = ask[16 * j : 16 * j + 16]
 
     pl.semaphore_wait(barrier, 22)
     asks = []
     for j in range(1, 8):
-        copy = remote(ask_send.at[j], ask_mid.at[j], ask1_s.at[j], ask1_r.at[j], zc_plus(j))
-        copy.start()
-        asks.append(copy)
+        asks.append(start(remote(ask_send.at[j], ask_mid.at[j], ask1_s.at[j], ask1_r.at[j], zc_plus(j))))
     ask_mid[0] = ask_send[0]
 
     for k in range(4):
@@ -139,14 +152,15 @@
 
     for copy in asks:
         copy.wait_recv()
+    group = lax.broadcasted_iota(I32, (16, 128), 1) // CAP
+    merged = ask_mid[0]
+    for j in range(1, 8):
+        merged = jnp.where(group == j, ask_mid[j], merged)
     for i in range(16):
-        for j in range(8):
-            ask_mid2[i, pl.ds(j, 1), :] = ask_mid[j, pl.ds(i, 1), :]
+        ask_mid2[i] = merged[i : i + 1]
     asks2 = []
     for i in range(1, 16):
-        copy = remote(ask_mid2.at[i], ask_got.at[i], ask2_s.at[i], ask2_r.at[i], yx_plus(i))
-        copy.start()
-        asks2.append(copy)
+        asks2.append(start(remote(ask_mid2.at[i], ask_got.at[i], ask2_s.at[i], ask2_r.at[i], yx_plus(i))))
     ask_got[0] = ask_mid2[0]
 
     for b in range(8):
@@ -167,12 +181,13 @@
         copy.wait_recv()
     to_smem = pltpu.make_async_copy(ask_got, ask_smem, smem_sem)
     to_smem.start()
-    row_ids[...] = ask_got[...]
+    for i in range(16):
+        row_ids[:, 8 * CAP * i : 8 * CAP * i + 8 * CAP] = ask_got[i][:, : 8 * CAP]
     to_smem.wait()
 
     def look_up(i, j, out):
         for c in range(CAP):
-            asked = jnp.clip(ask_smem[i, j, c], 0, ROWS - 1)
+            asked = jnp.clip(ask_smem[i, 0, CAP * j + c], 0, ROWS - 1)
             stage[j, pl.ds(c, 1), :] = tab32[pl.ds(asked, 1), :]
         for q in range(3):
             out[q] = stage[j, 4 * q : 4 * q + 4, :].astype(BF16)
@@ -193,20 +208,24 @@
         send_rows(0, j)
     look_up(0, 0, rows_got.at[0])
 
+    rest = pl.ds(1, DEVS - 1)
+    sent.append(pltpu.make_async_copy(rows_send.at[rest], rows_send.at[rest], row_s).wait)
     for k in (4, 5):
         loads[k].wait()
-    rest = pl.ds(1, DEVS - 1)
     pltpu.make_async_copy(rows_got.at[rest], rows_got.at[rest], row_r).wait()
 
-    @pl.loop(0, 32)
-    def _(g):
-        for a in range(4):
-            for q in range(3):
-                pack[12 * a + 4 * q : 12 * a + 4 * q + 4, :] = rows_got[g * 4 + a, q].astype(F32)
-        fetched[pl.ds(pl.multiple_of(g * 48, 16), 48), :] = pack[...].astype(BF16)
+    def unpack(got):
+        @pl.loop(0, 32)
+        def _(g):
+            for a in range(4):
+                for q in range(3):
+                    pack[12 * a + 4 * q : 12 * a + 4 * q + 4, :] = got[g * 4 + a, q].astype(F32)
+            fetched[pl.ds(pl.multiple_of(g * 48, 16), 48), :] = pack[...].astype(BF16)
+
+    unpack(rows_got)
 
     local32[...] = jnp.zeros_like(local32)
-    head = w_head[...].astype(F32)
+    head = w_head[...].reshape(1, HID).astype(F32)
     small = [jnp.zeros((1, HID), F32)] * 3
     for m in range(2):
         at = slice(256 * m, 256 * m + 256)
@@ -302,7 +321,7 @@
         return remote(at, at, agc_s.at[l, k], agc_r.at[l, k], sibling)
 
     for l in range(3):
-        core_copy(l).start()
+        start(core_copy(l))
 
     for m in range(2):
         at = slice(256 * m, 256 * m + 256)
@@ -335,7 +354,7 @@
             half0[l, at] = total.astype(BF16)
 
         for k in (2, 1, 3):
-            rs1_copy(l, k).start()
+            start(rs1_copy(l, k))
 
     def grad_copy(i, j):
         r = i * 8 + j
@@ -351,6 +370,7 @@
     for j in ZC_ORDER[:-1]:
         grad_copy(0, j).start()
     incoming[0] = grads_send[0]
+    sent.append(pltpu.make_async_copy(grads_send.at[rest], grads_send.at[rest], grad_s).wait)
 
     for l in range(3):
         for k in range(1, 4):
@@ -363,7 +383,20 @@
             sum1[l, at] = total
             half1[l, at] = total.astype(BF16)
         for k in (2, 1, 3):
-            rs2_copy(l, k).start()
+            start(rs2_copy(l, k))
+
+    pltpu.make_async_copy(incoming.at[rest], incoming.at[rest], grad_r).wait()
+    unpack(incoming)
+
+    def update(quarter):
+        for half in range(2):
+            base = quarter * 2048 + half * 1024
+            here_row = lax.broadcasted_iota(I32, (1024, SLOTS), 0) + base
+            hot_rows[...] = jnp.where(here_row == row_ids[...], 1.0, 0.0).astype(BF16)
+            at = slice(base, base + 1024)
+            tab32[at, :] = tab32[at, :] - 8.0 * dot(hot_rows[...], fetched[...])
+
+    update(0)
     for l in range(3):
         for k in range(1, 4):
             rs2_copy(l, k).wait_recv()
@@ -373,7 +406,8 @@
         half2[l] = total.astype(BF16)
         got3[l, here[lanes[l][2]]] = total.astype(BF16)
         for k in (2, 1, 3):
-            x3_copy(l, k).start()
+            start(x3_copy(l, k))
+    update(1)
     for l in range(3):
         for k in range(1, 4):
             x3_copy(l, k).wait_recv()
@@ -382,33 +416,24 @@
             total = total + got3[l, a].astype(F32)
         gathered[pl.ds(unit_at(mc, l, here[lanes[l][0]], here[lanes[l][1]]), PIECE)] = total.astype(BF16)
         for k in (2, 1, 3):
-            ag2_copy(l, k).start()
+            start(ag2_copy(l, k))
+    update(2)
     for l in range(3):
         for k in range(1, 4):
             ag2_copy(l, k).wait_recv()
         for k in (2, 1, 3):
-            ag1_copy(l, k).start()
-        agc_copy(l, 0).start()
+            start(ag1_copy(l, k))
+        start(agc_copy(l, 0))
+    update(3)
     for l in range(3):
         for k in (1, 3, 2):
             ag1_copy(l, k).wait_recv()
-            agc_copy(l, k).start()
+            start(agc_copy(l, k))
     for l in range(3):
         for k in range(4):
             agc_copy(l, k).wait_recv()
-    pltpu.make_async_copy(incoming.at[rest], incoming.at[rest], grad_r).wait()
-
-    for copy in asks + asks2:
-        copy.wait_send()
-    pltpu.make_async_copy(rows_send.at[rest], rows_send.at[rest], row_s).wait()
-    pltpu.make_async_copy(grads_send.at[rest], grads_send.at[rest], grad_s).wait()
-    for l in range(3):
-        core_copy(l).wait_send()
-        for k in range(1, 4):
-            for copy in (rs1_copy, rs2_copy, x3_copy, ag2_copy, ag1_copy):
-                copy(l, k).wait_send()
-        for k in range(4):
-            agc_copy(l, k).wait_send()
+
+    flush()
 
 
 def step(owners, rows, labels, table, w_first, bias_first, w_second, bias_second, w_head, head_bias):
@@ -416,15 +441,17 @@
     any_ = pl.BlockSpec(memory_space=pl.ANY)
     dma = pltpu.SemaphoreType.DMA
     scratch = [
+        pltpu.VMEM((DEVS, 3, 4, EMB), BF16),
+        pltpu.VMEM((1, SLOTS), I32),
+        pltpu.VMEM((1024, SLOTS), BF16),
         pltpu.VMEM((ROWS, EMB), BF16),
-        pltpu.VMEM((ROWS, EMB), F32),
         pltpu.VMEM((IN, HID), BF16),
         pltpu.VMEM((HID, HID), BF16),
         pltpu.VMEM((8, 16, 128), I32),
         pltpu.VMEM((8, 16, 128), I32),
-        pltpu.VMEM((16, 8, 128), I32),
-        pltpu.VMEM((16, 8, 128), I32),
-        pltpu.SMEM((16, 8, 128), I32),
+        pltpu.VMEM((16, 1, 128), I32),
+        pltpu.VMEM((16, 1, 128), I32),
+        pltpu.SMEM((16, 1, 128), I32),
         pltpu.VMEM((8, 1, 128), I32),
         pltpu.VMEM((PAIRS, 128), F32),
         pltpu.VMEM((2 * PAIRS, SLOTS), BF16),
@@ -458,96 +485,78 @@
     ]
     return pl.pallas_call(
         step_kernel,
-        out_shape=(
-            jax.ShapeDtypeStruct((DEVS, 3, 4, EMB), BF16),
-            jax.ShapeDtypeStruct((16, 8, 128), I32),
-            jax.ShapeDtypeStruct((UNITS, 8, 128), BF16),
-        ),
+        out_shape=(pltpu.VMEM((ROWS, EMB), F32), pltpu.VMEM((UNITS, 8, 128), BF16)),
         in_specs=[vmem, vmem, vmem, any_, any_, vmem, any_, vmem, vmem, pl.BlockSpec(memory_space=pltpu.SMEM)],
-        out_specs=(vmem, vmem, vmem),
+        out_specs=(vmem, vmem),
         scratch_shapes=scratch,
         compiler_params=pltpu.CompilerParams(
-            collective_id=0, has_side_effects=True, vmem_limit_bytes=56 << 20
+            collective_id=0, has_side_effects=True, vmem_limit_bytes=VMEM_STEP
         ),
         name="exchange_and_mlp",
     )(owners, rows, labels, table, w_first, bias_first, w_second, bias_second, w_head, head_bias)
 
 
-BLOCK = 1024
-
-
-def update_kernel(
-    table, incoming, ids, units_first, units_second, units_small,
-    new_table, grad_first, grad_second, grad_small,
-    pack, grads,
+def finish_kernel(
+    table, units, new_table, grad_first, grad_second, grad_small, first32, second32, table_sem, grad_sem
 ):
-    step = pl.program_id(0)
-
-    @pl.when(step == 0)
-    def _():
-        @pl.loop(0, 32)
-        def _(g):
-            for a in range(4):
-                for q in range(3):
-                    pack[12 * a + 4 * q : 12 * a + 4 * q + 4, :] = incoming[g * 4 + a, q].astype(F32)
-            grads[pl.ds(pl.multiple_of(g * 48, 16), 48), :] = pack[...].astype(BF16)
-
+    parts = [
+        pltpu.make_async_copy(
+            table.at[pl.ds(k * 1024, 1024)], new_table.at[pl.ds(k * 1024, 1024)], table_sem.at[k]
+        )
+        for k in range(8)
+    ]
+    for part in parts:
+        part.start()
+    for array, out, first_unit in ((first32, grad_first, 0), (second32, grad_second, UNITS_FIRST)):
+
+        @pl.loop(0, array.shape[0] // 32)
+        def _(t):
+            for u in range(4):
+                at = pl.ds(pl.multiple_of(t * 32 + u * 8, 8), 8)
+                for c in range(4):
+                    array[at, 128 * c : 128 * c + 128] = units[first_unit + t * 16 + u * 4 + c].astype(F32)
+
+        part = pltpu.make_async_copy(array, out, grad_sem.at[len(parts) - 8])
+        part.start()
+        parts.append(part)
     for c in range(4):
-        for t in range(12):
-            grad_first[8 * t : 8 * t + 8, 128 * c : 128 * c + 128] = units_first[4 * t + c].astype(F32)
-        for t in range(8):
-            grad_second[8 * t : 8 * t + 8, 128 * c : 128 * c + 128] = units_second[4 * t + c].astype(F32)
-        grad_small[:, 128 * c : 128 * c + 128] = units_small[c].astype(F32)[0:3]
-
-    @pl.loop(0, BLOCK // 256)
-    def _(t):
-        at = pl.ds(pl.multiple_of(t * 256, 256), 256)
-        here = lax.broadcasted_iota(I32, (256, SLOTS), 0) + (step * BLOCK + t * 256)
-        hot = jnp.where(here == ids[...], 1.0, 0.0).astype(BF16)
-        new_table[at, :] = table[at, :].astype(F32) - 8.0 * dot(hot, grads[...])
-
-
-def update(table, incoming, ids, units):
-    steps = ROWS // BLOCK
+        grad_small[:, 128 * c : 128 * c + 128] = units[640 + c].astype(F32)[0:3]
+    for part in parts:
+        part.wait()
+
+
+def finish(table, units):
+    vmem = pl.BlockSpec(memory_space=pltpu.VMEM)
+    any_ = pl.BlockSpec(memory_space=pl.ANY)
     return pl.pallas_call(
-        update_kernel,
-        grid=(steps,),
-        in_specs=[
-            pl.BlockSpec((BLOCK, EMB), lambda s: (s, 0)),
-            pl.BlockSpec((DEVS, 3, 4, EMB), lambda s: (0, 0, 0, 0)),
-            pl.BlockSpec((1, SLOTS), lambda s: (0, 0)),
-            pl.BlockSpec((UNITS_FIRST // steps, 8, 128), lambda s: (s, 0, 0)),
-            pl.BlockSpec((UNITS_SECOND // steps, 8, 128), lambda s: (12 + s, 0, 0)),
-            pl.BlockSpec((4, 8, 128), lambda s: (160, 0, 0)),
-        ],
-        out_specs=(
-            pl.BlockSpec((BLOCK, EMB), lambda s: (s, 0)),
-            pl.BlockSpec((IN // steps, HID), lambda s: (s, 0)),
-            pl.BlockSpec((HID // steps, HID), lambda s: (s, 0)),
-            pl.BlockSpec((3, HID), lambda s: (0, 0)),
-        ),
+        finish_kernel,
+        in_specs=[vmem, vmem],
+        out_specs=(any_, any_, any_, vmem),
         out_shape=(
             jax.ShapeDtypeStruct((ROWS, EMB), F32),
             jax.ShapeDtypeStruct((IN, HID), F32),
             jax.ShapeDtypeStruct((HID, HID), F32),
             jax.ShapeDtypeStruct((3, HID), F32),
         ),
-        scratch_shapes=[pltpu.VMEM((48, EMB), F32), pltpu.VMEM((SLOTS, EMB), BF16)],
-        compiler_params=pltpu.CompilerParams(vmem_limit_bytes=48 << 20),
-        name="scatter_update",
-    )(table, incoming, ids, units, units, units)
+        scratch_shapes=[
+            pltpu.VMEM((IN, HID), F32),
+            pltpu.VMEM((HID, HID), F32),
+            pltpu.SemaphoreType.DMA((8,)),
+            pltpu.SemaphoreType.DMA((2,)),
+        ],
+        compiler_params=pltpu.CompilerParams(vmem_limit_bytes=8 << 20),
+        name="write_out",
+    )(pltpu.with_memory_space_constraint(table, pltpu.VMEM), pltpu.with_memory_space_constraint(units, pltpu.VMEM))
 
 
 def on_device(
     node_table, owners, local_rows, labels, w_first, bias_first, w_second, bias_second, w_head, head_bias
 ):
-    incoming, row_ids, units = step(
+    table, units = step(
         owners.T, local_rows.T, labels.reshape(1, PAIRS), node_table,
-        w_first, bias_first.reshape(1, HID), w_second, bias_second.reshape(1, HID),
-        w_head.reshape(1, HID), head_bias,
+        w_first, bias_first.reshape(1, HID), w_second, bias_second.reshape(1, HID), w_head, head_bias,
     )
-    ids = row_ids[:, :, :CAP].reshape(1, SLOTS)
-    return update(node_table, incoming, ids, units)
+    return finish(table, units)
 
 
 def solution(mesh):

time: 93.2 us -> 77.2 us (0.83)
  Pallas kernels: 87 us -> 75.7 us
  local copies, waits for them, and re-layouts: 4.67 us -> 0 us
    pallas_call x2, Pallas kernels: 87 us -> 75.7 us  [the longest x1 71 us: step(): pl.pallas_call(step_kernel, out_shape=(pltpu.VMEM((ROWS, EMB), F32), pltp...]
    unnamed x4 -> x0, local copies, waits for them, and re-layouts: 2.47 us -> none
    reshape x2 -> x0, local copies, waits for them, and re-layouts: 2.21 us -> none  [the longest x1 1.26 us: on_device(): w_head.reshape(1, HID)]
where the time goes in v2:
time: 77.2 us; the launch traced here: 77 us
  Pallas kernels  75.7 us (98%)
  between operations  1.29 us (2%)
    pallas_call x1, Pallas kernels, step(): pl.pallas_call(step_kernel, out_shape=(pltpu.VMEM((ROWS, EMB), F32), pltp...  71 us
    pallas_call x1, Pallas kernels, finish(): pl.pallas_call(finish_kernel, in_specs=[vmem, vmem], out_specs=(any_, any...  4.77 us

profile of v2, /device:TPU:1, one launch (start us, length us, event | category | flops | bytes accessed | tf_op | source)
XLA Modules:
  0.0 77.0 jit_solution(11759167053554856940)
XLA Ops:
  1.3 71.0 %exchange_and_mlp.1 = (f32[8192,256]{1,0:T(8,128)S(1)}, bf16[672,8,128]{2,1,0:T(8,128)(2,1)S(1)}) custom-call(s32[2,512]{1,0:T(2,128)} %bitcast.5, s32[2,512]{1,0:T(2,128)} %bitcast.6, s32[1,512]{1,0:T(1,128)} %bitcast.7, bf16[8192,256]{1,0:T(8,128)(2,1)} %table.1, bf16[768,512]{1,0:T(8,128)(2,1)} %w_first.1, f32[1,512]{1,0:T(1,128)} %bitcast.8, ...), custom_call_target="tpu_custom_call" | custom-call | tf_op jit(solution)/shard_map/exchange_and_mlp/pallas_call | solution.py:486
  72.3 4.8 %write_out.1 = (f32[8192,256]{1,0:T(8,128)}, f32[768,512]{1,0:T(8,128)}, f32[512,512]{1,0:T(8,128)}, f32[3,512]{1,0:T(4,128)}) custom-call(f32[8192,256]{1,0:T(8,128)S(1)} %get-tuple-element.6.table, bf16[672,8,128]{2,1,0:T(8,128)(2,1)S(1)} %get-tuple-element.7.units), custom_call_target="tpu_custom_call" | custom-call | tf_op jit(solution)/shard_map/write_out/pallas_call | solution.py:531

commit v3 on v2

--- a/solution.py
+++ b/solution.py
@@ -32,11 +32,15 @@
     return ((y * 4 + x) * 4 + z) * 2 + c
 
 
-def far_first(k):
-    return 2 + k - 3 * (k // 2) - 2 * (k // 3)
-
-
+FAR = ((2, 2), (2, 1), (2, 3), (1, 2), (3, 2), (1, 1), (3, 3), (1, 3), (3, 1), (2, 0), (0, 2), (1, 0), (3, 0), (0, 1), (0, 3), (0, 0))
+ODD = tuple((y, x) for y, x in FAR if (y + x) % 2)
+EVEN = tuple((y, x) for y, x in FAR if (y + x) % 2 == 0)
+AG1_ORDER = ((2, 0), (2, 1), (1, 0), (3, 0), (1, 1), (3, 1), (0, 1))
 ZC_ORDER = (4, 5, 2, 3, 6, 7, 1, 0)
+
+
+def place_of(y, x):
+    return (y + x) % 2 * 8 + y * 2 + x // 2
 
 
 def remote(src, dst, send, recv, to):
@@ -54,7 +58,7 @@
     feat, hid1, del1, del2, one_hot_grads, out32, grads_send,
     local32, local16, got_core, sum0, half0, got1, sum1, half1, got2, half2, got3,
     load_sem, ask1_s, ask1_r, ask2_s, ask2_r, smem_sem, row_s, row_r, grad_s, grad_r,
-    core_s, core_r, rs1_s, rs1_r, rs2_s, rs2_r, x3_s, x3_r, ag2_s, ag2_r, ag1_s, ag1_r, agc_s, agc_r,
+    core_s, core_r, rs1_s, rs1_r, rs2_s, rs2_r, x3_s, x3_r, ag2_s, ag2_r, ag1_s, ag1_r,
 ):
     me = lax.axis_index("dev")
     my, mx, mz, mc = me // 32, me // 8 % 4, me // 2 % 4, me % 2
@@ -73,8 +77,8 @@
 
     sent = []
 
-    def flush():
-        for wait in sent:
+    def flush(waits):
+        for wait in waits:
             wait()
 
     def start(copy):
@@ -105,8 +109,9 @@
     d_x = ((own >> 3) - mx) & 3
     d_z = ((own >> 1) - mz) & 3
     d_c = (own - mc) & 1
-    d_yx, d_zc = d_y * 4 + d_x, d_z * 2 + d_c
-    ask_bucket, bucket = d_zc * 16 + d_yx, d_yx * 8 + d_zc
+    d_zc = d_z * 2 + d_c
+    ask_bucket = d_zc * 16 + d_y * 4 + d_x
+    bucket = (((d_y + d_x) & 1) * 8 + d_y * 2 + (d_x >> 1)) * 8 + d_zc
     row = rows[...]
     row_hi, row_lo = (row >> 6).astype(F32), (row & 63).astype(F32)
     sub = lax.broadcasted_iota(I32, (128, 128), 0)
@@ -142,14 +147,16 @@
         asks.append(start(remote(ask_send.at[j], ask_mid.at[j], ask1_s.at[j], ask1_r.at[j], zc_plus(j))))
     ask_mid[0] = ask_send[0]
 
-    for k in range(4):
-        loads[k].wait()
-
-        @pl.loop(0, 32)
-        def _(t):
-            at = pl.ds(pl.multiple_of(k * 2048 + t * 64, 64), 64)
-            tab32[at, :] = tab16[at, :].astype(F32)
-
+    def widen(begin, end):
+        for k in range(begin, end):
+            loads[k].wait()
+
+            @pl.loop(0, 16)
+            def _(t):
+                at = pl.ds(pl.multiple_of(k * 2048 + t * 128, 128), 128)
+                tab32[at, :] = tab16[at, :].astype(F32)
+
+    widen(0, 2)
     for copy in asks:
         copy.wait_recv()
     group = lax.broadcasted_iota(I32, (16, 128), 1) // CAP
@@ -163,26 +170,14 @@
         asks2.append(start(remote(ask_mid2.at[i], ask_got.at[i], ask2_s.at[i], ask2_r.at[i], yx_plus(i))))
     ask_got[0] = ask_mid2[0]
 
-    for b in range(8):
-        slot_b = slot_row[b]
-        column = jnp.transpose(jnp.broadcast_to(slot_b.astype(F32), (128, 128))).astype(I32)
-
-        @pl.loop(0, 12)
-        def _(k):
-            at = pl.ds(pl.multiple_of(k * 128, 128), 128)
-            pick[128 * b : 128 * b + 128, at] = jnp.where(column == lane + k * 128, 1.0, 0.0).astype(BF16)
-            place[at, 128 * b : 128 * b + 128] = jnp.where(sub + k * 128 == slot_b, 1.0, 0.0).astype(BF16)
-
-    for b in range(4):
-        part = labels[:, 128 * b : 128 * b + 128].astype(F32)
-        label_col[128 * b : 128 * b + 128, :] = jnp.transpose(jnp.broadcast_to(part, (128, 128)))
-
+    widen(2, 4)
     for copy in asks2:
         copy.wait_recv()
     to_smem = pltpu.make_async_copy(ask_got, ask_smem, smem_sem)
     to_smem.start()
-    for i in range(16):
-        row_ids[:, 8 * CAP * i : 8 * CAP * i + 8 * CAP] = ask_got[i][:, : 8 * CAP]
+    for y, x in FAR:
+        at = 8 * CAP * place_of(y, x)
+        row_ids[:, at : at + 8 * CAP] = ask_got[y * 4 + x][:, : 8 * CAP]
     to_smem.wait()
 
     def look_up(i, j, out):
@@ -192,21 +187,37 @@
         for q in range(3):
             out[q] = stage[j, 4 * q : 4 * q + 4, :].astype(BF16)
 
-    def send_rows(i, j):
-        r = i * 8 + j
-        look_up(i, j, rows_send.at[r])
-        remote(rows_send.at[r], rows_got.at[r], row_s, row_r, minus(i, j)).start()
-
-    def rows_of(t, carry):
-        i = far_first(t // 4) * 4 + far_first(t % 4)
+    def send_rows(y, x, j):
+        r = place_of(y, x) * 8 + j
+        look_up(y * 4 + x, j, rows_send.at[r])
+        remote(rows_send.at[r], rows_got.at[r], row_s, row_r, minus(y * 4 + x, j)).start()
+
+    def column(_, digits):
         for j in ZC_ORDER:
-            send_rows(i, j)
-        return carry
-
-    lax.fori_loop(0, 15, rows_of, 0)
+            send_rows(digits % 16 // 4, digits % 4, j)
+        return digits // 16
+
+    for part in (FAR[:7], FAR[7:14]):
+        lax.fori_loop(0, 7, column, sum((y * 4 + x) * 16**n for n, (y, x) in enumerate(part)))
+    for j in ZC_ORDER:
+        send_rows(*FAR[14], j)
     for j in ZC_ORDER[:-1]:
-        send_rows(0, j)
+        send_rows(0, 0, j)
     look_up(0, 0, rows_got.at[0])
+
+    for b in range(8):
+        slot_b = slot_row[b]
+        column = jnp.transpose(jnp.broadcast_to(slot_b.astype(F32), (128, 128))).astype(I32)
+
+        @pl.loop(0, 12)
+        def _(k):
+            at = pl.ds(pl.multiple_of(k * 128, 128), 128)
+            pick[128 * b : 128 * b + 128, at] = jnp.where(column == lane + k * 128, 1.0, 0.0).astype(BF16)
+            place[at, 128 * b : 128 * b + 128] = jnp.where(sub + k * 128 == slot_b, 1.0, 0.0).astype(BF16)
+
+    for b in range(4):
+        part = labels[:, 128 * b : 128 * b + 128].astype(F32)
+        label_col[128 * b : 128 * b + 128, :] = jnp.transpose(jnp.broadcast_to(part, (128, 128)))
 
     rest = pl.ds(1, DEVS - 1)
     sent.append(pltpu.make_async_copy(rows_send.at[rest], rows_send.at[rest], row_s).wait)
@@ -214,15 +225,15 @@
         loads[k].wait()
     pltpu.make_async_copy(rows_got.at[rest], rows_got.at[rest], row_r).wait()
 
-    def unpack(got):
-        @pl.loop(0, 32)
+    def unpack(got, begin, end):
+        @pl.loop(begin // 4, end // 4)
         def _(g):
             for a in range(4):
                 for q in range(3):
                     pack[12 * a + 4 * q : 12 * a + 4 * q + 4, :] = got[g * 4 + a, q].astype(F32)
             fetched[pl.ds(pl.multiple_of(g * 48, 16), 48), :] = pack[...].astype(BF16)
 
-    unpack(rows_got)
+    unpack(rows_got, 0, DEVS)
 
     local32[...] = jnp.zeros_like(local32)
     head = w_head[...].reshape(1, HID).astype(F32)
@@ -250,6 +261,47 @@
             small[2] + jnp.sum(hidden_second * dlogit, axis=0, keepdims=True),
         ]
 
+    for c in range(4):
+        for k in range(3):
+            local32[640 + c, k : k + 1, :] = small[k][:, 128 * c : 128 * c + 128]
+        local16[640 + c] = local32[640 + c].astype(BF16)
+
+    for m in range(2):
+        at = slice(256 * m, 256 * m + 256)
+        grad_input = nt(del1[at, :], w1[...])
+        grad_product = grad_input[:, 2 * EMB :]
+        grad_one = grad_input[:, :EMB] + grad_product * feat[at, EMB : 2 * EMB].astype(F32)
+        grad_two = grad_input[:, EMB : 2 * EMB] + grad_product * feat[at, 0:EMB].astype(F32)
+        one_hot_grads[256 * m : 256 * m + 256, :] = grad_one.astype(BF16)
+        one_hot_grads[PAIRS + 256 * m : PAIRS + 256 * m + 256, :] = grad_two.astype(BF16)
+
+    @pl.loop(0, 4)
+    def _(k):
+        at = pl.ds(pl.multiple_of(k * 384, 128), 384)
+        out32[...] = dot(place[at, :], one_hot_grads[...])
+        for r in range(32):
+            for q in range(3):
+                grads_send[k * 32 + r, q] = out32[12 * r + 4 * q : 12 * r + 4 * q + 4, :].astype(BF16)
+
+    halves_at = (pl.ds(DEVS // 2, DEVS // 2), pl.ds(1, DEVS // 2 - 1))
+
+    def send_grads(half, columns):
+        for y, x in columns:
+            for j in ZC_ORDER:
+                r = place_of(y, x) * 8 + j
+                if r:
+                    copy = remote(
+                        grads_send.at[r], incoming.at[r], grad_s.at[half], grad_r.at[half], plus(y * 4 + x, j)
+                    )
+                    copy.start()
+
+    def sent_grads(half):
+        at = grads_send.at[halves_at[half]]
+        sent.append(pltpu.make_async_copy(at, at, grad_s.at[half]).wait)
+
+    incoming[0] = grads_send[0]
+    send_grads(0, ODD)
+    sent_grads(0)
     def put(unit, value):
         local32[unit] = value
         local16[unit] = value.astype(BF16)
@@ -267,19 +319,15 @@
                     UNITS_FIRST + block * 128 + t * 4 + c,
                     grad[8 * t : 8 * t + 8, 128 * c : 128 * c + 128],
                 )
-    for c in range(4):
-        for k in range(3):
-            local32[640 + c, k : k + 1, :] = small[k][:, 128 * c : 128 * c + 128]
-        local16[640 + c] = local32[640 + c].astype(BF16)
     for u in range(644, UNITS):
         local16[u] = jnp.zeros((8, 128), BF16)
 
     here = {"y": my, "x": mx, "z": mz}
 
-    def along(axis, k):
+    def along(axis, k, other=0):
         at = dict(here)
         at[axis] = (at[axis] + k) % 4
-        return device(at["y"], at["x"], at["z"], mc)
+        return device(at["y"], at["x"], at["z"], (mc + other) % 2)
 
     sibling = device(my, mx, mz, 1 - mc)
     lanes = (("y", "x", "z"), ("x", "z", "y"), ("z", "y", "x"))
@@ -312,33 +360,27 @@
         at = gathered.at[pl.ds(unit_at(mc, l, a, b), span2)]
         return remote(at, at, ag2_s.at[l, k], ag2_r.at[l, k], along(lanes[l][1], k))
 
-    def ag1_copy(l, k):
+    def ag1_copy(l, k, other):
         at = gathered.at[pl.ds(unit_at(mc, l, here[lanes[l][0]]), span1)]
-        return remote(at, at, ag1_s.at[l, k], ag1_r.at[l, k], along(lanes[l][0], k))
-
-    def agc_copy(l, k):
-        at = gathered.at[pl.ds(unit_at(mc, l, (here[lanes[l][0]] + 4 - k) % 4), span1)]
-        return remote(at, at, agc_s.at[l, k], agc_r.at[l, k], sibling)
+        to = along(lanes[l][0], k, other)
+        return remote(at, at, ag1_s.at[l, k + 4 * other], ag1_r.at[l, k + 4 * other], to)
 
     for l in range(3):
         start(core_copy(l))
 
-    for m in range(2):
-        at = slice(256 * m, 256 * m + 256)
-        grad_input = nt(del1[at, :], w1[...])
-        grad_product = grad_input[:, 2 * EMB :]
-        grad_one = grad_input[:, :EMB] + grad_product * feat[at, EMB : 2 * EMB].astype(F32)
-        grad_two = grad_input[:, EMB : 2 * EMB] + grad_product * feat[at, 0:EMB].astype(F32)
-        one_hot_grads[256 * m : 256 * m + 256, :] = grad_one.astype(BF16)
-        one_hot_grads[PAIRS + 256 * m : PAIRS + 256 * m + 256, :] = grad_two.astype(BF16)
-
-    @pl.loop(0, 4)
-    def _(k):
-        at = pl.ds(pl.multiple_of(k * 384, 128), 384)
-        out32[...] = dot(place[at, :], one_hot_grads[...])
-        for r in range(32):
-            for q in range(3):
-                grads_send[k * 32 + r, q] = out32[12 * r + 4 * q : 12 * r + 4 * q + 4, :].astype(BF16)
+    def wait_grads(half):
+        at = incoming.at[halves_at[half]]
+        pltpu.make_async_copy(at, at, grad_r.at[half]).wait()
+        unpack(incoming, DEVS // 2 * (1 - half), DEVS // 2 * (2 - half))
+
+    def update(half, part):
+        slots = slice(SLOTS // 2 * (1 - half), SLOTS // 2 * (2 - half))
+        for block in range(4):
+            base = part * 4096 + block * 1024
+            here_row = lax.broadcasted_iota(I32, (1024, SLOTS // 2), 0) + base
+            hot_rows[...] = jnp.where(here_row == row_ids[:, slots], 1.0, 0.0).astype(BF16)
+            at = slice(base, base + 1024)
+            tab32[at, :] = tab32[at, :] - 8.0 * dot(hot_rows[...], fetched[slots, :])
 
     for l in range(3):
         core_copy(l).wait_recv()
@@ -355,22 +397,6 @@
 
         for k in (2, 1, 3):
             start(rs1_copy(l, k))
-
-    def grad_copy(i, j):
-        r = i * 8 + j
-        return remote(grads_send.at[r], incoming.at[r], grad_s, grad_r, plus(i, j))
-
-    def grads_of(t, carry):
-        i = far_first(t // 4) * 4 + far_first(t % 4)
-        for j in ZC_ORDER:
-            grad_copy(i, j).start()
-        return carry
-
-    lax.fori_loop(0, 15, grads_of, 0)
-    for j in ZC_ORDER[:-1]:
-        grad_copy(0, j).start()
-    incoming[0] = grads_send[0]
-    sent.append(pltpu.make_async_copy(grads_send.at[rest], grads_send.at[rest], grad_s).wait)
 
     for l in range(3):
         for k in range(1, 4):
@@ -384,19 +410,10 @@
             half1[l, at] = total.astype(BF16)
         for k in (2, 1, 3):
             start(rs2_copy(l, k))
-
-    pltpu.make_async_copy(incoming.at[rest], incoming.at[rest], grad_r).wait()
-    unpack(incoming)
-
-    def update(quarter):
-        for half in range(2):
-            base = quarter * 2048 + half * 1024
-            here_row = lax.broadcasted_iota(I32, (1024, SLOTS), 0) + base
-            hot_rows[...] = jnp.where(here_row == row_ids[...], 1.0, 0.0).astype(BF16)
-            at = slice(base, base + 1024)
-            tab32[at, :] = tab32[at, :] - 8.0 * dot(hot_rows[...], fetched[...])
-
-    update(0)
+    send_grads(1, EVEN[:3])
+
+    wait_grads(0)
+    update(0, 0)
     for l in range(3):
         for k in range(1, 4):
             rs2_copy(l, k).wait_recv()
@@ -407,7 +424,8 @@
         got3[l, here[lanes[l][2]]] = total.astype(BF16)
         for k in (2, 1, 3):
             start(x3_copy(l, k))
-    update(1)
+    send_grads(1, EVEN[3:6])
+    update(0, 1)
     for l in range(3):
         for k in range(1, 4):
             x3_copy(l, k).wait_recv()
@@ -417,23 +435,23 @@
         gathered[pl.ds(unit_at(mc, l, here[lanes[l][0]], here[lanes[l][1]]), PIECE)] = total.astype(BF16)
         for k in (2, 1, 3):
             start(ag2_copy(l, k))
-    update(2)
+    send_grads(1, EVEN[6:])
+    sent_grads(1)
+    early, sent[:] = list(sent), []
     for l in range(3):
         for k in range(1, 4):
             ag2_copy(l, k).wait_recv()
-        for k in (2, 1, 3):
-            start(ag1_copy(l, k))
-        start(agc_copy(l, 0))
-    update(3)
-    for l in range(3):
-        for k in (1, 3, 2):
-            ag1_copy(l, k).wait_recv()
-            start(agc_copy(l, k))
-    for l in range(3):
-        for k in range(4):
-            agc_copy(l, k).wait_recv()
-
-    flush()
+        for k, other in AG1_ORDER:
+            start(ag1_copy(l, k, other))
+    flush(early)
+    wait_grads(1)
+    update(1, 0)
+    update(1, 1)
+    for l in range(3):
+        for k, other in AG1_ORDER:
+            ag1_copy(l, k, other).wait_recv()
+
+    flush(sent)
 
 
 def step(owners, rows, labels, table, w_first, bias_first, w_second, bias_second, w_head, head_bias):
@@ -443,7 +461,7 @@
     scratch = [
         pltpu.VMEM((DEVS, 3, 4, EMB), BF16),
         pltpu.VMEM((1, SLOTS), I32),
-        pltpu.VMEM((1024, SLOTS), BF16),
+        pltpu.VMEM((1024, SLOTS // 2), BF16),
         pltpu.VMEM((ROWS, EMB), BF16),
         pltpu.VMEM((IN, HID), BF16),
         pltpu.VMEM((HID, HID), BF16),
@@ -479,9 +497,9 @@
         pltpu.VMEM((3, 4, PIECE, 8, 128), BF16),
         pltpu.VMEM((3, PIECE, 8, 128), BF16),
         pltpu.VMEM((3, 4, PIECE, 8, 128), BF16),
-        dma((6,)), dma((8,)), dma((8,)), dma((16,)), dma((16,)), dma, dma, dma, dma, dma,
+        dma((6,)), dma((8,)), dma((8,)), dma((16,)), dma((16,)), dma, dma, dma, dma((2,)), dma((2,)),
         dma((3,)), dma((3,)), dma((3, 4)), dma((3, 4)), dma((3, 4)), dma((3, 4)), dma((3, 4)), dma((3, 4)),
-        dma((3, 4)), dma((3, 4)), dma((3, 4)), dma((3, 4)), dma((3, 4)), dma((3, 4)),
+        dma((3, 4)), dma((3, 4)), dma((3, 8)), dma((3, 8)),
     ]
     return pl.pallas_call(
         step_kernel,

time: 77.2 us -> 74.4 us (0.964)
  Pallas kernels: 75.7 us -> 72.8 us
    pallas_call x1, Pallas kernels: 71 us -> 68.1 us  [step(): pl.pallas_call(step_kernel, out_shape=(pltpu.VMEM((ROWS, EMB), F32), pltp...]
where the time goes in v3:
time: 74.4 us; the launch traced here: 74.3 us
  Pallas kernels  72.8 us (98%)
  between operations  1.45 us (2%)
    pallas_call x1, Pallas kernels, step(): pl.pallas_call(step_kernel, out_shape=(pltpu.VMEM((ROWS, EMB), F32), pltp...  68.1 us
    pallas_call x1, Pallas kernels, finish(): pl.pallas_call(finish_kernel, in_specs=[vmem, vmem], out_specs=(any_, any...  4.77 us

profile of v3, /device:TPU:1, one launch (start us, length us, event | category | flops | bytes accessed | tf_op | source)
XLA Modules:
  0.0 74.3 jit_solution(18383898038523726791)
XLA Ops:
  1.3 68.1 %exchange_and_mlp.1 = (f32[8192,256]{1,0:T(8,128)S(1)}, bf16[672,8,128]{2,1,0:T(8,128)(2,1)S(1)}) custom-call(s32[2,512]{1,0:T(2,128)} %bitcast.5, s32[2,512]{1,0:T(2,128)} %bitcast.6, s32[1,512]{1,0:T(1,128)} %bitcast.7, bf16[8192,256]{1,0:T(8,128)(2,1)} %table.1, bf16[768,512]{1,0:T(8,128)(2,1)} %w_first.1, f32[1,512]{1,0:T(1,128)} %bitcast.8, ...), custom_call_target="tpu_custom_call" | custom-call | tf_op jit(solution)/shard_map/exchange_and_mlp/pallas_call | solution.py:504
  69.3 4.8 %write_out.1 = (f32[8192,256]{1,0:T(8,128)}, f32[768,512]{1,0:T(8,128)}, f32[512,512]{1,0:T(8,128)}, f32[3,512]{1,0:T(4,128)}) custom-call(f32[8192,256]{1,0:T(8,128)S(1)} %get-tuple-element.6.table, bf16[672,8,128]{2,1,0:T(8,128)(2,1)S(1)} %get-tuple-element.7.units), custom_call_target="tpu_custom_call" | custom-call | tf_op jit(solution)/shard_map/write_out/pallas_call | solution.py:549

commit v4 on v3

--- a/solution.py
+++ b/solution.py
@@ -39,6 +39,10 @@
 ZC_ORDER = (4, 5, 2, 3, 6, 7, 1, 0)
 
 
+def unit_place(v):
+    return v % 224 // 112 * (UNITS // 2) + v // 224 * 112 + v % 112
+
+
 def place_of(y, x):
     return (y + x) % 2 * 8 + y * 2 + x // 2
 
@@ -54,7 +58,7 @@
     tab32, gathered,
     incoming, row_ids, hot_rows, tab16, w1, w2,
     ask_send, ask_mid, ask_mid2, ask_got, ask_smem, slot_row, label_col,
-    pick, place, stage, rows_send, rows_got, pack, fetched,
+    pick, picked, place, stage, rows_send, rows_got, pack, fetched,
     feat, hid1, del1, del2, one_hot_grads, out32, grads_send,
     local32, local16, got_core, sum0, half0, got1, sum1, half1, got2, half2, got3,
     load_sem, ask1_s, ask1_r, ask2_s, ask2_r, smem_sem, row_s, row_r, grad_s, grad_r,
@@ -190,17 +194,19 @@
     def send_rows(y, x, j):
         r = place_of(y, x) * 8 + j
         look_up(y * 4 + x, j, rows_send.at[r])
-        remote(rows_send.at[r], rows_got.at[r], row_s, row_r, minus(y * 4 + x, j)).start()
+        half = 1 - (y + x) % 2
+        remote(rows_send.at[r], rows_got.at[r], row_s, row_r.at[half], minus(y * 4 + x, j)).start()
 
     def column(_, digits):
         for j in ZC_ORDER:
             send_rows(digits % 16 // 4, digits % 4, j)
         return digits // 16
 
-    for part in (FAR[:7], FAR[7:14]):
+    columns = ODD + EVEN[:-1]
+    for part in (columns[:7], columns[7:14]):
         lax.fori_loop(0, 7, column, sum((y * 4 + x) * 16**n for n, (y, x) in enumerate(part)))
     for j in ZC_ORDER:
-        send_rows(*FAR[14], j)
+        send_rows(*columns[14], j)
     for j in ZC_ORDER[:-1]:
         send_rows(0, 0, j)
     look_up(0, 0, rows_got.at[0])
@@ -223,8 +229,6 @@
     sent.append(pltpu.make_async_copy(rows_send.at[rest], rows_send.at[rest], row_s).wait)
     for k in (4, 5):
         loads[k].wait()
-    pltpu.make_async_copy(rows_got.at[rest], rows_got.at[rest], row_r).wait()
-
     def unpack(got, begin, end):
         @pl.loop(begin // 4, end // 4)
         def _(g):
@@ -233,15 +237,25 @@
                     pack[12 * a + 4 * q : 12 * a + 4 * q + 4, :] = got[g * 4 + a, q].astype(F32)
             fetched[pl.ds(pl.multiple_of(g * 48, 16), 48), :] = pack[...].astype(BF16)
 
-    unpack(rows_got, 0, DEVS)
+    def wait_rows(half):
+        at = rows_got.at[halves_at[half]]
+        pltpu.make_async_copy(at, at, row_r.at[half]).wait()
+        unpack(rows_got, DEVS // 2 * (1 - half), DEVS // 2 * (2 - half))
+
+    halves_at = (pl.ds(DEVS // 2, DEVS // 2), pl.ds(1, DEVS // 2 - 1))
+    lower, upper = slice(0, SLOTS // 2), slice(SLOTS // 2, SLOTS)
+    wait_rows(0)
+    picked[...] = dot(pick[:, upper], fetched[upper, :])
+    wait_rows(1)
 
     local32[...] = jnp.zeros_like(local32)
     head = w_head[...].reshape(1, HID).astype(F32)
     small = [jnp.zeros((1, HID), F32)] * 3
     for m in range(2):
         at = slice(256 * m, 256 * m + 256)
-        first = dot(pick[256 * m : 256 * m + 256, :], fetched[...])
-        second = dot(pick[PAIRS + 256 * m : PAIRS + 256 * m + 256, :], fetched[...])
+        at2 = slice(PAIRS + 256 * m, PAIRS + 256 * m + 256)
+        first = picked[at, :] + dot(pick[at, lower], fetched[lower, :])
+        second = picked[at2, :] + dot(pick[at2, lower], fetched[lower, :])
         feat[at, 0:EMB] = first.astype(BF16)
         feat[at, EMB : 2 * EMB] = second.astype(BF16)
         feat[at, 2 * EMB :] = (first * second).astype(BF16)
@@ -263,8 +277,72 @@
 
     for c in range(4):
         for k in range(3):
-            local32[640 + c, k : k + 1, :] = small[k][:, 128 * c : 128 * c + 128]
-        local16[640 + c] = local32[640 + c].astype(BF16)
+            local32[unit_place(640 + c), k : k + 1, :] = small[k][:, 128 * c : 128 * c + 128]
+        local16[unit_place(640 + c)] = local32[unit_place(640 + c)].astype(BF16)
+
+    here = {"y": my, "x": mx, "z": mz}
+
+    def along(axis, k, other=0):
+        at = dict(here)
+        at[axis] = (at[axis] + k) % 4
+        return device(at["y"], at["x"], at["z"], (mc + other) % 2)
+
+    sibling = device(my, mx, mz, 1 - mc)
+    lanes = (("y", "x", "z"), ("x", "z", "y"), ("z", "y", "x"))
+    span1, span2 = 4 * PIECE, PIECE
+    lane_units = 16 * PIECE
+
+    def core_copy(l):
+        at = pl.ds((1 - mc) * (UNITS // 2) + l * lane_units, lane_units)
+        return remote(local16.at[at], got_core.at[l], core_s.at[l], core_r.at[l], sibling)
+
+    def rs1_copy(l, k):
+        axis = lanes[l][0]
+        at = pl.ds((here[axis] + k) % 4 * span1, span1)
+        return remote(half0.at[l, at], got1.at[l, k], rs1_s.at[l, k], rs1_r.at[l, k], along(axis, k))
+
+    def rs2_copy(l, k):
+        axis = lanes[l][1]
+        at = pl.ds((here[axis] + k) % 4 * span2, span2)
+        return remote(half1.at[l, at], got2.at[l, k], rs2_s.at[l, k], rs2_r.at[l, k], along(axis, k))
+
+    def x3_copy(l, k):
+        axis = lanes[l][2]
+        return remote(half2.at[l], got3.at[l, here[axis]], x3_s.at[l, k], x3_r.at[l, k], along(axis, k))
+
+    def unit_at(core, l, one, two=0):
+        return core * (UNITS // 2) + l * lane_units + one * span1 + two * span2
+
+    def ag2_copy(l, k):
+        a, b = here[lanes[l][0]], here[lanes[l][1]]
+        at = gathered.at[pl.ds(unit_at(mc, l, a, b), span2)]
+        return remote(at, at, ag2_s.at[l, k], ag2_r.at[l, k], along(lanes[l][1], k))
+
+    def ag1_copy(l, k, other):
+        at = gathered.at[pl.ds(unit_at(mc, l, here[lanes[l][0]]), span1)]
+        to = along(lanes[l][0], k, other)
+        return remote(at, at, ag1_s.at[l, k + 4 * other], ag1_r.at[l, k + 4 * other], to)
+
+    def put(v, value):
+        unit = unit_place(v)
+        local32[unit] = value
+        local16[unit] = value.astype(BF16)
+
+    def put_block(first, grad):
+        for n in range(32):
+            for c in range(4):
+                put(first + n * 4 + c, grad[8 * n : 8 * n + 8, 128 * c : 128 * c + 128])
+
+    for u in range(644, UNITS):
+        local16[unit_place(u)] = jnp.zeros((8, 128), BF16)
+    for block in range(3):
+        put_block(block * 128, tn(feat[:, 256 * block : 256 * block + 256], del1[...]))
+        if block == 1:
+            start(core_copy(0))
+    for block in range(2):
+        put_block(UNITS_FIRST + block * 128, tn(hid1[:, 256 * block : 256 * block + 256], del2[...]))
+        start(core_copy(1 + block))
+
 
     for m in range(2):
         at = slice(256 * m, 256 * m + 256)
@@ -282,8 +360,6 @@
         for r in range(32):
             for q in range(3):
                 grads_send[k * 32 + r, q] = out32[12 * r + 4 * q : 12 * r + 4 * q + 4, :].astype(BF16)
-
-    halves_at = (pl.ds(DEVS // 2, DEVS // 2), pl.ds(1, DEVS // 2 - 1))
 
     def send_grads(half, columns):
         for y, x in columns:
@@ -300,88 +376,21 @@
         sent.append(pltpu.make_async_copy(at, at, grad_s.at[half]).wait)
 
     incoming[0] = grads_send[0]
-    send_grads(0, ODD)
-    sent_grads(0)
-    def put(unit, value):
-        local32[unit] = value
-        local16[unit] = value.astype(BF16)
-
-    for block in range(3):
-        grad = tn(feat[:, 256 * block : 256 * block + 256], del1[...])
-        for t in range(32):
-            for c in range(4):
-                put(block * 128 + t * 4 + c, grad[8 * t : 8 * t + 8, 128 * c : 128 * c + 128])
-    for block in range(2):
-        grad = tn(hid1[:, 256 * block : 256 * block + 256], del2[...])
-        for t in range(32):
-            for c in range(4):
-                put(
-                    UNITS_FIRST + block * 128 + t * 4 + c,
-                    grad[8 * t : 8 * t + 8, 128 * c : 128 * c + 128],
-                )
-    for u in range(644, UNITS):
-        local16[u] = jnp.zeros((8, 128), BF16)
-
-    here = {"y": my, "x": mx, "z": mz}
-
-    def along(axis, k, other=0):
-        at = dict(here)
-        at[axis] = (at[axis] + k) % 4
-        return device(at["y"], at["x"], at["z"], (mc + other) % 2)
-
-    sibling = device(my, mx, mz, 1 - mc)
-    lanes = (("y", "x", "z"), ("x", "z", "y"), ("z", "y", "x"))
-    span1, span2 = 4 * PIECE, PIECE
-    lane_units = 16 * PIECE
-
-    def core_copy(l):
-        at = pl.ds((1 - mc) * (UNITS // 2) + l * lane_units, lane_units)
-        return remote(local16.at[at], got_core.at[l], core_s.at[l], core_r.at[l], sibling)
-
-    def rs1_copy(l, k):
-        axis = lanes[l][0]
-        at = pl.ds((here[axis] + k) % 4 * span1, span1)
-        return remote(half0.at[l, at], got1.at[l, k], rs1_s.at[l, k], rs1_r.at[l, k], along(axis, k))
-
-    def rs2_copy(l, k):
-        axis = lanes[l][1]
-        at = pl.ds((here[axis] + k) % 4 * span2, span2)
-        return remote(half1.at[l, at], got2.at[l, k], rs2_s.at[l, k], rs2_r.at[l, k], along(axis, k))
-
-    def x3_copy(l, k):
-        axis = lanes[l][2]
-        return remote(half2.at[l], got3.at[l, here[axis]], x3_s.at[l, k], x3_r.at[l, k], along(axis, k))
-
-    def unit_at(core, l, one, two=0):
-        return core * (UNITS // 2) + l * lane_units + one * span1 + two * span2
-
-    def ag2_copy(l, k):
-        a, b = here[lanes[l][0]], here[lanes[l][1]]
-        at = gathered.at[pl.ds(unit_at(mc, l, a, b), span2)]
-        return remote(at, at, ag2_s.at[l, k], ag2_r.at[l, k], along(lanes[l][1], k))
-
-    def ag1_copy(l, k, other):
-        at = gathered.at[pl.ds(unit_at(mc, l, here[lanes[l][0]]), span1)]
-        to = along(lanes[l][0], k, other)
-        return remote(at, at, ag1_s.at[l, k + 4 * other], ag1_r.at[l, k + 4 * other], to)
-
-    for l in range(3):
-        start(core_copy(l))
-
     def wait_grads(half):
         at = incoming.at[halves_at[half]]
         pltpu.make_async_copy(at, at, grad_r.at[half]).wait()
         unpack(incoming, DEVS // 2 * (1 - half), DEVS // 2 * (2 - half))
 
-    def update(half, part):
+    def update(half, begin, end):
         slots = slice(SLOTS // 2 * (1 - half), SLOTS // 2 * (2 - half))
-        for block in range(4):
-            base = part * 4096 + block * 1024
+        for base in range(begin * 1024, end * 1024, 1024):
             here_row = lax.broadcasted_iota(I32, (1024, SLOTS // 2), 0) + base
             hot_rows[...] = jnp.where(here_row == row_ids[:, slots], 1.0, 0.0).astype(BF16)
             at = slice(base, base + 1024)
             tab32[at, :] = tab32[at, :] - 8.0 * dot(hot_rows[...], fetched[slots, :])
 
+    send_grads(0, ODD)
+    sent_grads(0)
     for l in range(3):
         core_copy(l).wait_recv()
 
@@ -410,10 +419,10 @@
             half1[l, at] = total.astype(BF16)
         for k in (2, 1, 3):
             start(rs2_copy(l, k))
-    send_grads(1, EVEN[:3])
+    send_grads(1, EVEN[:4])
 
     wait_grads(0)
-    update(0, 0)
+    update(0, 0, 3)
     for l in range(3):
         for k in range(1, 4):
             rs2_copy(l, k).wait_recv()
@@ -424,8 +433,8 @@
         got3[l, here[lanes[l][2]]] = total.astype(BF16)
         for k in (2, 1, 3):
             start(x3_copy(l, k))
-    send_grads(1, EVEN[3:6])
-    update(0, 1)
+    send_grads(1, EVEN[4:])
+    update(0, 3, 6)
     for l in range(3):
         for k in range(1, 4):
             x3_copy(l, k).wait_recv()
@@ -435,9 +444,9 @@
         gathered[pl.ds(unit_at(mc, l, here[lanes[l][0]], here[lanes[l][1]]), PIECE)] = total.astype(BF16)
         for k in (2, 1, 3):
             start(ag2_copy(l, k))
-    send_grads(1, EVEN[6:])
     sent_grads(1)
     early, sent[:] = list(sent), []
+    update(0, 6, 8)
     for l in range(3):
         for k in range(1, 4):
             ag2_copy(l, k).wait_recv()
@@ -445,8 +454,7 @@
             start(ag1_copy(l, k, other))
     flush(early)
     wait_grads(1)
-    update(1, 0)
-    update(1, 1)
+    update(1, 0, 8)
     for l in range(3):
         for k, other in AG1_ORDER:
             ag1_copy(l, k, other).wait_recv()
@@ -473,6 +481,7 @@
         pltpu.VMEM((8, 1, 128), I32),
         pltpu.VMEM((PAIRS, 128), F32),
         pltpu.VMEM((2 * PAIRS, SLOTS), BF16),
+        pltpu.VMEM((2 * PAIRS, EMB), F32),
         pltpu.VMEM((SLOTS, 2 * PAIRS), BF16),
         pltpu.VMEM((8, 16, EMB), F32),
         pltpu.VMEM((DEVS, 3, 4, EMB), BF16),
@@ -497,7 +506,7 @@
         pltpu.VMEM((3, 4, PIECE, 8, 128), BF16),
         pltpu.VMEM((3, PIECE, 8, 128), BF16),
         pltpu.VMEM((3, 4, PIECE, 8, 128), BF16),
-        dma((6,)), dma((8,)), dma((8,)), dma((16,)), dma((16,)), dma, dma, dma, dma((2,)), dma((2,)),
+        dma((6,)), dma((8,)), dma((8,)), dma((16,)), dma((16,)), dma, dma, dma((2,)), dma((2,)), dma((2,)),
         dma((3,)), dma((3,)), dma((3, 4)), dma((3, 4)), dma((3, 4)), dma((3, 4)), dma((3, 4)), dma((3, 4)),
         dma((3, 4)), dma((3, 4)), dma((3, 8)), dma((3, 8)),
     ]
@@ -532,13 +541,13 @@
             for u in range(4):
                 at = pl.ds(pl.multiple_of(t * 32 + u * 8, 8), 8)
                 for c in range(4):
-                    array[at, 128 * c : 128 * c + 128] = units[first_unit + t * 16 + u * 4 + c].astype(F32)
+                    array[at, 128 * c : 128 * c + 128] = units[unit_place(first_unit + t * 16) + u * 4 + c].astype(F32)
 
         part = pltpu.make_async_copy(array, out, grad_sem.at[len(parts) - 8])
         part.start()
         parts.append(part)
     for c in range(4):
-        grad_small[:, 128 * c : 128 * c + 128] = units[640 + c].astype(F32)[0:3]
+        grad_small[:, 128 * c : 128 * c + 128] = units[unit_place(640 + c)].astype(F32)[0:3]
     for part in parts:
         part.wait()
 

time: 74.4 us -> 73 us (0.981)
  Pallas kernels: 72.8 us -> 71.4 us
    pallas_call x1, Pallas kernels: 68.1 us -> 66.6 us  [step(): pl.pallas_call(step_kernel, out_shape=(pltpu.VMEM((ROWS, EMB), F32), pltp...]
where the time goes in v4:
time: 73 us; the launch traced here: 72.8 us
  Pallas kernels  71.4 us (98%)
  between operations  1.45 us (2%)
    pallas_call x1, Pallas kernels, step(): pl.pallas_call(step_kernel, out_shape=(pltpu.VMEM((ROWS, EMB), F32), pltp...  66.6 us
    pallas_call x1, Pallas kernels, finish(): pl.pallas_call(finish_kernel, in_specs=[vmem, vmem], out_specs=(any_, any...  4.77 us

profile of v4, /device:TPU:1, one launch (start us, length us, event | category | flops | bytes accessed | tf_op | source)
XLA Modules:
  0.0 72.8 jit_solution(18149114358457553533)
XLA Ops:
  1.3 66.6 %exchange_and_mlp.1 = (f32[8192,256]{1,0:T(8,128)S(1)}, bf16[672,8,128]{2,1,0:T(8,128)(2,1)S(1)}) custom-call(s32[2,512]{1,0:T(2,128)} %bitcast.5, s32[2,512]{1,0:T(2,128)} %bitcast.6, s32[1,512]{1,0:T(1,128)} %bitcast.7, bf16[8192,256]{1,0:T(8,128)(2,1)} %table.1, bf16[768,512]{1,0:T(8,128)(2,1)} %w_first.1, f32[1,512]{1,0:T(1,128)} %bitcast.8, ...), custom_call_target="tpu_custom_call" | custom-call | tf_op jit(solution)/shard_map/exchange_and_mlp/pallas_call | solution.py:513
  67.9 4.8 %write_out.1 = (f32[8192,256]{1,0:T(8,128)}, f32[768,512]{1,0:T(8,128)}, f32[512,512]{1,0:T(8,128)}, f32[3,512]{1,0:T(4,128)}) custom-call(f32[8192,256]{1,0:T(8,128)S(1)} %get-tuple-element.6.table, bf16[672,8,128]{2,1,0:T(8,128)(2,1)S(1)} %get-tuple-element.7.units), custom_call_target="tpu_custom_call" | custom-call | tf_op jit(solution)/shard_map/write_out/pallas_call | solution.py:558

commit v5 on v4

--- a/solution.py
+++ b/solution.py
@@ -389,8 +389,6 @@
             at = slice(base, base + 1024)
             tab32[at, :] = tab32[at, :] - 8.0 * dot(hot_rows[...], fetched[slots, :])
 
-    send_grads(0, ODD)
-    sent_grads(0)
     for l in range(3):
         core_copy(l).wait_recv()
 
@@ -406,6 +404,8 @@
 
         for k in (2, 1, 3):
             start(rs1_copy(l, k))
+    send_grads(0, ODD)
+    sent_grads(0)
 
     for l in range(3):
         for k in range(1, 4):

time: 73 us -> 71.5 us (0.979)
  Pallas kernels: 71.4 us -> 69.9 us
    pallas_call x1, Pallas kernels: 66.6 us -> 65.1 us  [step(): pl.pallas_call(step_kernel, out_shape=(pltpu.VMEM((ROWS, EMB), F32), pltp...]
where the time goes in v5:
time: 71.5 us; the launch traced here: 71.3 us
  Pallas kernels  69.9 us (98%)
  between operations  1.45 us (2%)
    pallas_call x1, Pallas kernels, step(): pl.pallas_call(step_kernel, out_shape=(pltpu.VMEM((ROWS, EMB), F32), pltp...  65.1 us
    pallas_call x1, Pallas kernels, finish(): pl.pallas_call(finish_kernel, in_specs=[vmem, vmem], out_specs=(any_, any...  4.77 us

profile of v5, /device:TPU:1, one launch (start us, length us, event | category | flops | bytes accessed | tf_op | source)
XLA Modules:
  0.0 71.3 jit_solution(10510313495209283209)
XLA Ops:
  1.3 65.1 %exchange_and_mlp.1 = (f32[8192,256]{1,0:T(8,128)S(1)}, bf16[672,8,128]{2,1,0:T(8,128)(2,1)S(1)}) custom-call(s32[2,512]{1,0:T(2,128)} %bitcast.5, s32[2,512]{1,0:T(2,128)} %bitcast.6, s32[1,512]{1,0:T(1,128)} %bitcast.7, bf16[8192,256]{1,0:T(8,128)(2,1)} %table.1, bf16[768,512]{1,0:T(8,128)(2,1)} %w_first.1, f32[1,512]{1,0:T(1,128)} %bitcast.8, ...), custom_call_target="tpu_custom_call" | custom-call | tf_op jit(solution)/shard_map/exchange_and_mlp/pallas_call | solution.py:513
  66.4 4.8 %write_out.1 = (f32[8192,256]{1,0:T(8,128)}, f32[768,512]{1,0:T(8,128)}, f32[512,512]{1,0:T(8,128)}, f32[3,512]{1,0:T(4,128)}) custom-call(f32[8192,256]{1,0:T(8,128)S(1)} %get-tuple-element.6.table, bf16[672,8,128]{2,1,0:T(8,128)(2,1)S(1)} %get-tuple-element.7.units), custom_call_target="tpu_custom_call" | custom-call | tf_op jit(solution)/shard_map/write_out/pallas_call | solution.py:558
